TPU v7x, 128 devices: a whole 4x4x4 slice. The times are simulated.
128 devices in a mesh: dp: 8 (over x_lo, y), mp: 16 (over x_hi, z, core).
Axes of the slice: x: 4 (x_hi: 2, x_lo: 2; x = x_hi * 2 + x_lo), y: 4, z: 4, core: 2. Of those that a mesh axis runs over, the one named last changes fastest.
Arguments:
- grad_parts: float32 [8, 4096, 4096], P('dp', None, 'mp'), may hold values from -3 to 3
- home: int32 [8], replicated, may hold values from 0 to 7, each once
- left_stat: float32 [64, 512, 512], P('dp', 'mp'), may hold values from -3 to 3
- right_stat: float32 [64, 512, 512], P('dp', 'mp'), may hold values from -3 to 3
- left_root: bfloat16 [64, 512, 512], P('dp', 'mp'), may hold values from -0.5 to 1.5
- right_root: bfloat16 [64, 512, 512], P('dp', 'mp'), may hold values from -0.5 to 1.5
- first_moment: float32 [64, 512, 512], P('dp', 'mp'), may hold values from -2 to 2
- second_moment: float32 [64, 512, 512], P('dp', 'mp'), may hold values from 0.02 to 0.5
Outputs:
- new_left: float32 [64, 512, 512], P('dp', 'mp')
- new_right: float32 [64, 512, 512], P('dp', 'mp')
- new_first: float32 [64, 512, 512], P('dp', 'mp')
- new_second: float32 [64, 512, 512], P('dp', 'mp')
- update: bfloat16 [4096, 4096], P('dp', 'mp')
Inputs may be any that keep to these rules, and one draw needn't show every extreme that they name: Each block row is named once; block row r is owned by index home[r] // 1 of dp.
All inputs are finite; a program needn't handle non-finite values.
Results may differ from a plain program's by a relative error of at most 0.001.
Values may be sent and summed in bfloat16 or wider, within the bound.
A program may use at most 64 MiB of HBM per device.

v0:
```python
import jax
import jax.numpy as jnp
from jax import lax
from jax.sharding import PartitionSpec as P

HIGH = lax.Precision.HIGHEST
FIRST_DECAY = 0.9
SECOND_DECAY = 0.999
ADAM_EPS = 1e-08
NORM_EPS = 1e-06


def on_device(
    grad_parts, home, left_stat, right_stat, left_root, right_root, first_moment, second_moment
):
    partial_value = grad_parts[0]
    strip_cols = partial_value.shape[1]
    dp_count = lax.axis_size("dp")
    mp_count = lax.axis_size("mp")
    slot_count, slab_rows, block_size = left_stat.shape
    block_rows = partial_value.shape[0] // block_size
    per_owner = block_rows // dp_count
    col_blocks = slot_count // per_owner
    row_order = jnp.arange(block_rows, dtype=jnp.int32)
    source = jnp.sum(jnp.where(home[:, None] == row_order[None, :], row_order[:, None], 0), axis=0)
    picked_rows = (
        source.reshape(dp_count, 1, per_owner, 1) * block_size
        + jnp.arange(mp_count, dtype=jnp.int32).reshape(1, mp_count, 1, 1) * slab_rows
        + jnp.arange(slab_rows, dtype=jnp.int32).reshape(1, 1, 1, slab_rows)
    ).reshape(-1)
    ordered = jnp.take(partial_value, picked_rows, axis=0).reshape(
        dp_count * mp_count, per_owner, slab_rows, strip_cols
    )
    arrived = lax.all_to_all(ordered, ("dp", "mp"), split_axis=0, concat_axis=0, tiled=True)
    summed = jnp.sum(arrived.reshape(dp_count, mp_count, per_owner, slab_rows, strip_cols), axis=0)
    rows_mine = jnp.transpose(summed, (1, 2, 0, 3))
    block_view = rows_mine.reshape(per_owner, slab_rows, col_blocks, block_size)
    slot_grads = jnp.transpose(block_view, (0, 2, 1, 3)).reshape(slot_count, slab_rows, block_size)
    new_first = FIRST_DECAY * first_moment + (1.0 - FIRST_DECAY) * slot_grads
    new_second = SECOND_DECAY * second_moment + (1.0 - SECOND_DECAY) * slot_grads * slot_grads
    adam = new_first / (jnp.sqrt(new_second) + ADAM_EPS)
    adam_sums = jnp.sum(adam * adam, axis=(1, 2))
    my_start = lax.axis_index("mp") * slab_rows
    roots_left = left_root.astype(jnp.float32)
    shard_rows = lax.all_gather(slot_grads, "mp", axis=1, tiled=True)
    products = jnp.einsum("sik,sjk->sij", slot_grads, shard_rows, precision=HIGH)
    columns = lax.dynamic_slice_in_dim(shard_rows, my_start, slab_rows, 2)
    right_acc = jnp.einsum("sna,snj->saj", columns, shard_rows, precision=HIGH)
    absorb_left_applied = jnp.einsum("sin,snj->sij", roots_left, shard_rows, precision=HIGH)
    precond = jnp.einsum(
        "sin,snj->sij",
        absorb_left_applied,
        lax.all_gather(right_root, "mp", axis=1, tiled=True).astype(jnp.float32),
        precision=HIGH,
    )
    precond_sums = jnp.sum(precond * precond, axis=(1, 2))
    norm_sums = lax.psum((adam_sums, precond_sums), "mp")
    graft_scale = jnp.sqrt(norm_sums[0]) / (jnp.sqrt(norm_sums[1]) + NORM_EPS)
    update = (precond * graft_scale[:, None, None]).astype(jnp.bfloat16)
    strips_out = jnp.transpose(
        update.reshape(per_owner, col_blocks, slab_rows, block_size), (0, 2, 1, 3)
    )
    strips_out = strips_out.reshape(per_owner, slab_rows, mp_count, strip_cols)
    returned = lax.all_to_all(strips_out, "mp", split_axis=2, concat_axis=1, tiled=True)
    update_tile = returned.reshape(per_owner * block_size, strip_cols)
    return (left_stat + products, right_stat + right_acc, new_first, new_second, update_tile)


def solution(mesh):
    in_specs = (
        P("dp", None, "mp"),
        P(),
        P("dp", "mp", None),
        P("dp", "mp", None),
        P("dp", "mp", None),
        P("dp", "mp", None),
        P("dp", "mp", None),
        P("dp", "mp", None),
    )
    out_specs = (
        P("dp", "mp", None),
        P("dp", "mp", None),
        P("dp", "mp", None),
        P("dp", "mp", None),
        P("dp", "mp"),
    )
    return jax.shard_map(
        on_device, mesh=mesh, in_specs=in_specs, out_specs=out_specs, check_vma=False
    )
```

profile of v0, /device:TPU:1, one launch (start us, length us, event | category | flops | bytes accessed | tf_op | source)
XLA Modules:
  0.0 295.8 jit_solution(3987065655658480584)
XLA Ops:
  7.2 0.0 copy-start
  7.2 0.0 all-gather.6.cloned.1.call-start
  7.2 0.8 select_reduce_fusion
  8.0 0.1 broadcast_add_fusion
  8.1 0.2 add_reduce_fusion
  8.3 0.1 add.110
  8.4 0.1 add.119
  8.6 0.1 fusion.23
  8.7 18.3 %gather_fusion = f32[4096,256]{1,0:T(8,128)} fusion(f32[4096,256]{1,0:T(8,128)} %bitcast.57, s32[4096]{0:T(1024)S(1)} %broadcast_clamp_fusion), kind=kCustom, calls=%fused_computation | custom fusion | bytes 8404992 | tf_op jit(solution)/shard_map/jit(_take)/gather | solution.py:31
  26.9 3.4 %broadcast_select_fusion = f32[128,1,32,256]{3,2,1,0:T(8,128)S(1)} fusion(f32[128,1,32,256]{3,2,1,0:T(8,128)} %bitcast.58, pred[128,32]{1,0:T(8,128)(4,1)S(1)} %fusion.23), kind=kLoop, calls=%fused_computation.10 | loop fusion | flops 1048576 | bytes 8392704 | tf_op jit(solution)/shard_map/jit(_take)/select_n | solution.py:31
  30.3 63.3 %all_to_all.20 = f32[128,1,32,256]{3,2,1,0:T(8,128)S(1)} all-to-all(f32[128,1,32,256]{3,2,1,0:T(8,128)S(1)} %broadcast_select_fusion), channel_id=1, replica_groups=mesh['dp'=8,'mp'=16] {'dp','mp'}, dimensions={0} | all-to-all | bytes 8388608 | tf_op jit(solution)/shard_map/all_to_all | solution.py:34
  93.6 0.4 bitcast_reduce_fusion
  94.0 0.3 copy.27
  94.3 0.1 reshape.142
  94.5 1.1 copy.41
  95.6 0.0 all-gather.6.cloned.1.call-update
  95.6 0.0 all-gather.4.cloned.1.call-start
  95.7 0.7 all-gather.4.cloned.1.call-update
  96.4 1.5 multiply_reduce_fusion.1
  97.9 69.5 %all-gather.6.cloned.1.call-done = f32[1,8,512,512]{3,2,1,0:T(8,128)} async-done(((f32[1,8,32,512]{3,2,1,0:T(8,128)}), f32[1,8,512,512]{3,2,1,0:T(8,128)}) %all-gather.6.cloned.1.call-update) | async-done | bytes 8388624 | tf_op jit(solution)/shard_map/all_gather | solution.py:45
  167.3 6.4 %fusion.2 = f32[8,512,32]{1,2,0:T(8,128)S(1)} fusion(bf16[8,32,512]{2,1,0:T(8,128)(2,1)S(1)} %copy-done, f32[1,8,512,512]{3,2,1,0:T(8,128)} %all-gather.6.cloned.1.call-done), kind=kOutput, calls=%fused_computation.3 | convolution fusion | flops 805306368 | bytes 9175040 | tf_op jit(solution)/shard_map/sin,snj->sij/dot_general | solution.py:49
  173.7 49.3 %all-gather.4.cloned.1.call-done = bf16[8,512,512]{2,1,0:T(8,128)(2,1)} async-done(((bf16[8,32,512]{2,1,0:T(8,128)(2,1)}), bf16[8,512,512]{2,1,0:T(8,128)(2,1)}) %all-gather.4.cloned.1.call-update) | async-done | bytes 4194320 | tf_op jit(solution)/shard_map/all_gather | solution.py:53
  223.0 4.4 %multiply_reduce_fusion = (f32[8]{0:T(128)S(1)}, f32[8,32,512]{2,1,0:T(8,128)S(1)}) fusion(f32[8,512,32]{1,2,0:T(8,128)S(1)} %fusion.2, bf16[8,512,512]{2,1,0:T(8,128)(2,1)} %all-gather.4.cloned.1.call-done), kind=kOutput, calls=%fused_computation.19 | convolution fusion | flops 805568512 | bytes 5242912 | tf_op jit(solution)/shard_map/sin,snj->sij/dot_general | solution.py:50
  227.4 32.7 %all-reduce = (f32[8]{0:T(128)S(1)}, f32[8]{0:T(128)S(1)}) all-reduce(f32[8]{0:T(128)S(1)} %get-tuple-element.10, f32[8]{0:T(128)S(1)} %get-tuple-element.7), channel_id=1, replica_groups=mesh['dp'=8,'mp'=16] {'mp'}, use_global_device_ids=true, to_apply=%region_5.6 | all-reduce | flops 16 | bytes 128 | tf_op jit(solution)/shard_map/psum | solution.py:57
  260.2 0.1 fusion.20
  260.3 0.2 copy.30
  260.4 0.1 reshape.145
  260.5 0.8 copy.31
  261.3 5.9 %all-to-all-start.1 = ((bf16[1,32,16,256]{3,1,0,2:T(8,128)(2,1)}), bf16[1,32,16,256]{3,1,0,2:T(8,128)(2,1)S(1)}, u32[]{:S(2)}, u32[]{:S(2)}) async-start(bf16[1,32,16,256]{3,1,0,2:T(8,128)(2,1)} %copy.31), calls=%async_computation.1 | async-start | bytes 524288 | tf_op jit(solution)/shard_map/all_to_all | solution.py:64
  267.2 10.9 %fusion.8 = f32[8,32,512]{2,1,0:T(8,128)} fusion(f32[8,32,512]{2,1,0:T(8,128)S(1)} %copy-done.1, f32[1,8,512,512]{3,2,1,0:T(8,128)} %all-gather.6.cloned.1.call-done, f32[1,32,8,512]{3,2,1,0:T(8,128)S(1)} %reshape.142), kind=kOutput, calls=%fused_computation.11 | convolution fusion | flops 805437440 | bytes 9961472 | tf_op jit(solution)/shard_map/sik,sjk->sij/dot_general | solution.py:46
  278.1 10.1 %fusion.11 = f32[8,32,512]{2,1,0:T(8,128)} fusion(f32[8,32,512]{2,1,0:T(8,128)S(1)} %copy-done.2, f32[1,8,512,512]{3,2,1,0:T(8,128)} %all-gather.6.cloned.1.call-done, s32[]{:T(128)S(6)} %select_n.39), kind=kOutput, calls=%fused_computation.12 | convolution fusion | flops 805437440 | bytes 11534340 | tf_op jit(solution)/shard_map/sna,snj->saj/dot_general | solution.py:48
  288.3 0.7 copy.43
  (15 shorter events, 0.1 us)
Async XLA Ops:
  7.2 160.2 %copy-start = (bf16[8,32,512]{2,1,0:T(8,128)(2,1)S(1)}, bf16[8,32,512]{2,1,0:T(8,128)(2,1)}, u32[]{:S(2)}) copy-start(bf16[8,32,512]{2,1,0:T(8,128)(2,1)} %param.12) | copy-start | bytes 786436
  7.2 160.2 %all-gather.6.cloned.1.call-start = ((), (), s32[]{:S(2)}) async-start(), calls=%async_computation.3 | async-start | bytes 8912896 | tf_op jit(solution)/shard_map/all_gather | solution.py:45
  93.6 2.8 copy-start.3
  93.6 2.8 copy-start.4
  95.6 127.4 %all-gather.4.cloned.1.call-start = ((), (), s32[]{:S(2)}) async-start(), calls=%async_computation.2 | async-start | bytes 4456448 | tf_op jit(solution)/shard_map/all_gather | solution.py:53
  173.7 93.5 %copy-start.1 = (f32[8,32,512]{2,1,0:T(8,128)S(1)}, f32[8,32,512]{2,1,0:T(8,128)}, u32[]{:S(2)}) copy-start(f32[8,32,512]{2,1,0:T(8,128)} %param.10) | copy-start | bytes 1572868
  261.3 26.9 %all-to-all-start.1 = ((bf16[1,32,16,256]{3,1,0,2:T(8,128)(2,1)}), bf16[1,32,16,256]{3,1,0,2:T(8,128)(2,1)S(1)}, u32[]{:S(2)}, u32[]{:S(2)}) async-start(bf16[1,32,16,256]{3,1,0,2:T(8,128)(2,1)} %copy.31), calls=%async_computation.1 | async-start | bytes 524288 | tf_op jit(solution)/shard_map/all_to_all | solution.py:64
  267.2 10.9 %copy-start.2 = (f32[8,32,512]{2,1,0:T(8,128)S(1)}, f32[8,32,512]{2,1,0:T(8,128)}, u32[]{:S(2)}) copy-start(f32[8,32,512]{2,1,0:T(8,128)} %param.11) | copy-start | bytes 1572868
Sparse Core Ops, SparseCore 0:
  95.7 71.5 all-gather.5
  169.9 53.1 all-gather.3
where the time goes:
time: 296 us
  waiting for transfers between devices  119 us (40%)
  blocking collectives  96 us (32%)
  matrix products  31.8 us (11%)
  local copies, waits for them, and re-layouts  21.7 us (7%)
  between operations  14.2 us (5%)
  other arithmetic  6.64 us (2%)
  starting transfers between devices  5.96 us (2%)
    all_gather x1, waiting for transfers between devices, on_device(): shard_rows = lax.all_gather(slot_grads, 'mp', axis=1, tiled=True)  69.5 us
    all_to_all x1, blocking collectives, on_device(): lax.all_to_all(ordered, ('dp', 'mp'), split_axis=0, concat_axis=0, tiled=...  63.3 us
    all_gather x1, waiting for transfers between devices, on_device(): lax.all_gather(right_root, 'mp', axis=1, tiled=True).astype(jnp.float32)  49.3 us
    psum x1, blocking collectives, on_device(): norm_sums = lax.psum((adam_sums, precond_sums), 'mp')  32.7 us
    gather x1, local copies, waits for them, and re-layouts, on_device(): jnp.take(partial_value, picked_rows, axis=0)  18.3 us
    dot_general x1, matrix products, on_device(): jnp.einsum('sik,sjk->sij', slot_grads, shard_rows, precision=HIGH)  10.9 us
    dot_general x1, matrix products, on_device(): right_acc = jnp.einsum('sna,snj->saj', columns, shard_rows, precision=HIGH)  10.1 us
    dot_general x1, matrix products, on_device(): jnp.einsum('sin,snj->sij', roots_left, shard_rows, precision=HIGH)  6.39 us
  transfers between devices with their start and end apart: 3, of which 2 were waited for; matrix products, arithmetic and copies ran while one was open for 10% of the time, Pallas kernels for 0%

commit v1 on v0

v1 whole, which is shorter than its diff:
```python
import functools
import math

import jax
import jax.numpy as jnp
from jax import lax
from jax.experimental import pallas as pl
from jax.experimental.pallas import tpu as pltpu
from jax.sharding import PartitionSpec as P

FIRST_DECAY = 0.9
SECOND_DECAY = 0.999
ADAM_EPS = 1e-08
NORM_EPS = 1e-06
MESH = pl.DeviceIdType.MESH
F32 = jnp.float32
BF16 = jnp.bfloat16
I16 = jnp.int16
I32 = jnp.int32

B = 512
H = 256
S = 32
T = 16
LANES = 128
NB = 8
NY = 4
FULL = 32760.0
STEP = math.log(2.0) / 4.0
TINY = 1e-30

PEERS = [(a, b) for a in range(2) for b in range(4) if (a, b) != (0, 0)]


def code_of(peak):
    return jnp.ceil(jnp.log(jnp.maximum(peak, TINY)) * (1.0 / STEP))


def coded(x, code):
    return jnp.floor(x * (jnp.exp(code * -STEP) * FULL) + 0.5).astype(I32).astype(I16)


def scale_of(code):
    return jnp.exp(code.astype(I32).astype(F32) * STEP) * (1.0 / FULL)


def decoded(values, scale):
    return values.astype(I32).astype(F32) * scale


def encode_piece(read, out):
    for t in range(H // LANES):
        cols = pl.ds(t * LANES, LANES)
        x = read(cols).reshape(H // T, T, LANES)
        code = code_of(jnp.max(jnp.abs(x), axis=0))
        out[pl.ds(0, H), cols] = coded(x, code[None]).reshape(H, LANES)
        out[pl.ds(H, T), cols] = code.astype(I32).astype(I16)


def decode_piece(codes, cols):
    scale = scale_of(codes[pl.ds(H, T), cols])
    values = codes[pl.ds(0, H), cols].reshape(H // T, T, LANES)
    return decoded(values, scale[None]).reshape(H, LANES)


def encode_rows(x, out):
    n = B // LANES
    parts = [x[:, t * LANES : (t + 1) * LANES].reshape(S // T, T, LANES) for t in range(n)]
    peak = functools.reduce(jnp.maximum, [jnp.max(jnp.abs(p), axis=0) for p in parts])
    code = code_of(peak)
    for t in range(n):
        out[pl.ds(t * S, S), :] = coded(parts[t], code[None]).reshape(S, LANES)
    out[pl.ds(n * S, T), :] = code.astype(I32).astype(I16)


def decode_rows(codes):
    n = B // LANES
    scale = scale_of(codes[pl.ds(n * S, T), :])
    return [
        decoded(codes[pl.ds(t * S, S), :].reshape(S // T, T, LANES), scale[None]).reshape(S, LANES)
        for t in range(n)
    ]


def dot(a, b, dims=((1,), (0,))):
    return lax.dot_general(a, b, (dims, ((), ())), preferred_element_type=F32)


def split(x):
    high = x.astype(BF16)
    return high, (x - high.astype(F32)).astype(BF16)


def fold(x):
    r, c = x.shape
    x = jnp.sum(x.reshape(r // 8, 8, c), axis=0)
    return functools.reduce(jnp.add, [x[:, t * LANES : (t + 1) * LANES] for t in range(c // LANES)])


def kernel(
    home, part_hbm, left_hbm, right_hbm, lroot_hbm, rroot_hbm, first_hbm, second_hbm,
    new_left, new_right, new_first, new_second, update,
    part, left, right, first, second, lroot, rroot,
    x1_out, x1_in, y1_out, y1_in, x2_out, x2_in, y2_out, y2_in,
    acc, ghigh, glow, grow_out, grow_in, prod_out, prod_in, pright, precond,
    sums_out, sums_in, pair_out, pair_in,
    load_sem, root_send, root_recv, x1_send, x1_recv, y1_send, y1_recv, s2_send, s2_recv,
    core_send, core_recv, row_send, row_recv, sum_send, sum_recv,
):
    d = lax.axis_index("dp")
    m = lax.axis_index("mp")
    xl, y = d // NY, d % NY
    xh, z, k = m // 8, (m // 2) % 4, m % 2
    c = m // 2

    partner = (d, m + 1 - 2 * k)
    across = ((1 - xl) * NY + y, m)

    def along_y(j):
        return (xl * NY + (y + j) % NY, m)

    def chip_at(a, b):
        return ((xh + a) % 2) * 4 + (z + b) % 4

    def along_mp(a, b):
        return (d, chip_at(a, b) * 2 + k)

    def remote(src, dst, send, recv, device):
        return pltpu.make_async_remote_copy(
            src_ref=src, dst_ref=dst, send_sem=send, recv_sem=recv, device_id=device, device_id_type=MESH
        )

    loads = [
        pltpu.make_async_copy(src, dst, load_sem.at[i])
        for i, (src, dst) in enumerate(
            [
                (part_hbm, part), (left_hbm, left), (right_hbm, right), (first_hbm, first), (second_hbm, second),
                (lroot_hbm.at[c], lroot.at[c, k]), (rroot_hbm.at[c], rroot.at[c, k]),
            ]
        )
    ]
    loads[0].start()

    barrier = pltpu.get_barrier_semaphore()
    greeted = [partner, across] + [along_y(j) for j in (1, 2, 3)] + [along_mp(a, b) for a, b in PEERS]
    for device in greeted:
        pl.semaphore_signal(barrier, inc=1, device_id=device, device_id_type=MESH)
    pl.semaphore_wait(barrier, len(greeted))

    root_copies = []
    for i, (a, b) in enumerate(PEERS):
        there = chip_at(a, b)
        for w, (src, dst) in enumerate(((lroot_hbm, lroot), (rroot_hbm, rroot))):
            copy = remote(src.at[there], dst.at[c, k], root_send.at[w, i], root_recv.at[w, i], along_mp(a, b))
            copy.start()
            root_copies.append(copy)
    for load in loads[1:]:
        load.start()

    def source(q):
        return functools.reduce(jnp.maximum, [jnp.where(home[r] == q, r, 0) for r in range(NB)])

    def own_piece(q, half):
        row = source(q)
        return lambda cols: part[row, pl.ds(half * H, H), cols]

    def chunk(to_x, j):
        return to_x * NY + (y + j) % NY

    loads[0].wait()
    x1_copies, y1_copies = {}, {}

    def send_x1(j):
        encode_piece(own_piece(chunk(1 - xl, j), 1), x1_out.at[j])
        x1_copies[j] = remote(x1_out.at[j], x1_in.at[j], x1_send.at[j], x1_recv.at[j], across)
        x1_copies[j].start()

    def send_y1(w, j):
        to_x = 1 - xl if w == 0 else xl
        n = w * 3 + j - 1
        encode_piece(own_piece(chunk(to_x, j), 0), y1_out.at[n])
        y1_copies[w, j] = remote(y1_out.at[n], y1_in.at[n], y1_send.at[n], y1_recv.at[n], along_y(j))
        y1_copies[w, j].start()

    for j in (1, 2, 3):
        send_x1(j)
        send_y1(0, j)
    for j in (1, 2, 3):
        send_y1(1, j)
    send_x1(0)

    y2_copies = {}
    for j in (1, 2, 3):
        x1_copies[j].wait_recv()
        own = own_piece(chunk(xl, j), 1)
        encode_piece(lambda cols: own(cols) + decode_piece(x1_in.at[j], cols), y2_out.at[j - 1])
        y2_copies[j] = remote(y2_out.at[j - 1], y2_in.at[j - 1], s2_send.at[j], s2_recv.at[j], along_y(j))
        y2_copies[j].start()

    def y1_sum(w, read):
        def total(cols):
            out = read(cols)
            for j in (1, 2, 3):
                out = out + decode_piece(y1_in.at[w * 3 + j - 1], cols)
            return out

        return total

    for j in (1, 2, 3):
        y1_copies[0, j].wait_recv()
    encode_piece(y1_sum(0, own_piece(chunk(1 - xl, 0), 0)), x2_out)
    x2_copy = remote(x2_out, x2_in, s2_send.at[0], s2_recv.at[0], across)
    x2_copy.start()

    for copy in root_copies:
        copy.wait_recv()
    loads[5].wait()
    loads[6].wait()
    core_copies = []
    for w, ref in enumerate((lroot, rroot)):
        copy = remote(ref.at[:, k], ref.at[:, k], core_send.at[w], core_recv.at[w], partner)
        copy.start()
        core_copies.append(copy)

    halves = [pl.ds(t * LANES, LANES) for t in range(H // LANES)]
    x1_copies[0].wait_recv()
    own_low = own_piece(chunk(xl, 0), 1)
    for cols in halves:
        acc[pl.ds(H, H), cols] = own_low(cols) + decode_piece(x1_in.at[0], cols)
    for j in (1, 2, 3):
        y1_copies[1, j].wait_recv()
    own_high = y1_sum(1, own_piece(chunk(xl, 0), 0))
    for cols in halves:
        acc[pl.ds(0, H), cols] = own_high(cols)
    x2_copy.wait_recv()
    for j in (1, 2, 3):
        y2_copies[j].wait_recv()
    for t, cols in enumerate(halves):
        mine = pl.ds(pl.multiple_of(k * H + t * LANES, LANES), LANES)
        top = acc[pl.ds(0, H), cols] + decode_piece(x2_in, cols)
        high, low = split(top)
        ghigh[pl.ds(0, H), mine] = high
        glow[pl.ds(0, H), mine] = low
        bottom = acc[pl.ds(H, H), cols]
        for j in (1, 2, 3):
            bottom = bottom + decode_piece(y2_in.at[j - 1], cols)
        high, low = split(bottom)
        ghigh[pl.ds(H, H), mine] = high
        glow[pl.ds(H, H), mine] = low

    strip = pl.ds(pl.multiple_of(k * H, H), H)
    for w, ref in enumerate((ghigh, glow)):
        copy = remote(ref.at[:, strip], ref.at[:, strip], core_send.at[2 + w], core_recv.at[2 + w], partner)
        copy.start()
        core_copies.append(copy)
    core_copies[2].wait()
    core_copies[3].wait()

    def rows_for(there):
        return pl.ds(pl.multiple_of(there * 2 * S + k * S, S), S)

    row_copies = []
    for i, (a, b) in enumerate(PEERS + [(0, 0)]):
        there = chip_at(a, b)
        rows = rows_for(there)
        value = ghigh[rows, :].astype(F32) + glow[rows, :].astype(F32)
        if (a, b) == (0, 0):
            encode_rows(value, grow_in.at[c])
        else:
            encode_rows(value, grow_out.at[i])
            copy = remote(grow_out.at[i], grow_in.at[c], row_send.at[0, i], row_recv.at[0, i], along_mp(a, b))
            copy.start()
            row_copies.append(copy)

    high_rows = jnp.concatenate([ghigh[rows_for(t), :] for t in range(NB)], axis=0)
    low_rows = jnp.concatenate([glow[rows_for(t), :] for t in range(NB)], axis=0)
    nt = ((1,), (1,))
    product = dot(high_rows, ghigh[...], nt) + (dot(high_rows, glow[...], nt) + dot(low_rows, ghigh[...], nt))
    precond[...] = product.reshape(NB * S, B)
    prod_copies = []

    def send_products(w, read):
        for i, (a, b) in enumerate(PEERS + [(0, 0)]):
            value = read(chip_at(a, b))
            if (a, b) == (0, 0):
                encode_rows(value, prod_in.at[w, c])
            else:
                encode_rows(value, prod_out.at[w, i])
                copy = remote(
                    prod_out.at[w, i], prod_in.at[w, c], row_send.at[1 + w, i], row_recv.at[1 + w, i], along_mp(a, b)
                )
                copy.start()
                prod_copies.append(copy)

    send_products(0, lambda there: precond[pl.ds(pl.multiple_of(there * S, S), S), :])
    tn = ((0,), (0,))
    pright[...] = dot(ghigh[...], ghigh[...], tn) + (
        dot(ghigh[...], glow[...], tn) + dot(glow[...], ghigh[...], tn)
    )
    send_products(1, lambda there: pright[rows_for(there), :])

    core_copies[0].wait()
    core_copies[1].wait()
    rcols = jnp.concatenate(
        [rroot[a, b, :, strip] for a in range(NB) for b in range(2)], axis=0
    )
    inner = dot(ghigh[...], rcols) + dot(glow[...], rcols)
    inner_high, inner_low = split(inner)
    lrows = lroot[...].reshape(B, B)
    applied = dot(lrows, inner_high) + dot(lrows, inner_low)
    pright[:, pl.ds(0, H)] = applied
    pair_out[1] = fold(applied * applied)

    for i in (2, 1, 3, 4):
        loads[i].wait()
    for i, (a, b) in enumerate([(0, 0)] + PEERS):
        slot = chip_at(-a, -b)
        if i:
            row_copies[i - 1].wait_recv()
        total = jnp.zeros((8, LANES), F32)
        for t, grad in enumerate(decode_rows(grow_in.at[slot])):
            cols = pl.ds(t * LANES, LANES)
            mean = FIRST_DECAY * first[slot, :, cols] + (1.0 - FIRST_DECAY) * grad
            square = SECOND_DECAY * second[slot, :, cols] + (1.0 - SECOND_DECAY) * grad * grad
            new_first[slot, :, cols] = mean
            new_second[slot, :, cols] = square
            adam = mean / (jnp.sqrt(square) + ADAM_EPS)
            total = total + fold(adam * adam)
        sums_out[i] = total
    sum_copies = []
    for i, (a, b) in enumerate(PEERS):
        copy = remote(sums_out.at[i + 1], sums_in.at[i], sum_send.at[i], sum_recv.at[i], along_mp(-a, -b))
        copy.start()
        sum_copies.append(copy)

    for w, (old, new) in enumerate(((left, new_left), (right, new_right))):
        for i, (a, b) in enumerate([(0, 0)] + PEERS):
            slot = chip_at(-a, -b)
            if i:
                prod_copies[w * len(PEERS) + i - 1].wait_recv()
            for t, value in enumerate(decode_rows(prod_in.at[w, slot])):
                cols = pl.ds(t * LANES, LANES)
                new[slot, :, cols] = old[slot, :, cols] + value

    total = sums_out[0]
    for i, copy in enumerate(sum_copies):
        copy.wait_recv()
        total = total + sums_in[i]
    pair_out[0] = total
    pair_copy = remote(pair_out, pair_in, sum_send.at[len(PEERS)], sum_recv.at[len(PEERS)], partner)
    pair_copy.start()
    pair_copy.wait()
    norms = [jnp.sum(pair_out[w] + pair_in[w], axis=(0, 1), keepdims=True) for w in range(2)]
    graft = jnp.sqrt(norms[0]) / (jnp.sqrt(norms[1]) + NORM_EPS)
    update[...] = (pright[:, pl.ds(0, H)] * graft).astype(BF16)

    for copy in root_copies + row_copies + prod_copies + sum_copies:
        copy.wait_send()
    for copy in list(x1_copies.values()) + list(y1_copies.values()) + list(y2_copies.values()) + [x2_copy]:
        copy.wait_send()


def on_device(
    grad_parts, home, left_stat, right_stat, left_root, right_root, first_moment, second_moment
):
    in_hbm = pl.BlockSpec(memory_space=pltpu.HBM)
    vmem = pl.BlockSpec(memory_space=pltpu.VMEM)
    n = len(PEERS)
    piece = (H + T, H)
    rows = (S * B // LANES + T, LANES)
    dma = pltpu.SemaphoreType.DMA
    scratch = [
        pltpu.VMEM((NB, B, H), F32),
        *[pltpu.VMEM((NB, S, B), F32)] * 4,
        *[pltpu.VMEM((NB, 2, S, B), BF16)] * 2,
        *[pltpu.VMEM((4, *piece), I16)] * 2,
        *[pltpu.VMEM((6, *piece), I16)] * 2,
        *[pltpu.VMEM(piece, I16)] * 2,
        *[pltpu.VMEM((3, *piece), I16)] * 2,
        pltpu.VMEM((B, H), F32),
        *[pltpu.VMEM((B, B), BF16)] * 2,
        pltpu.VMEM((n, *rows), I16),
        pltpu.VMEM((NB, *rows), I16),
        pltpu.VMEM((2, n, *rows), I16),
        pltpu.VMEM((2, NB, *rows), I16),
        pltpu.VMEM((B, B), F32),
        pltpu.VMEM((H, B), F32),
        pltpu.VMEM((NB, 8, LANES), F32),
        pltpu.VMEM((n, 8, LANES), F32),
        *[pltpu.VMEM((2, 8, LANES), F32)] * 2,
        dma((7,)),
        *[dma((2, n))] * 2,
        *[dma((4,))] * 2,
        *[dma((6,))] * 2,
        *[dma((4,))] * 2,
        *[dma((4,))] * 2,
        *[dma((3, n))] * 2,
        *[dma((n + 1,))] * 2,
    ]
    rows_out = jax.ShapeDtypeStruct((NB, S, B), F32)
    return pl.pallas_call(
        kernel,
        out_shape=(rows_out,) * 4 + (jax.ShapeDtypeStruct((B, H), BF16),),
        in_specs=[pl.BlockSpec(memory_space=pltpu.SMEM)] + [in_hbm] * 7,
        out_specs=[vmem] * 5,
        scratch_shapes=scratch,
        compiler_params=pltpu.CompilerParams(
            collective_id=0, has_side_effects=True, vmem_limit_bytes=48 * 2**20
        ),
        cost_estimate=pl.CostEstimate(flops=2 * 10**9, bytes_accessed=9 * 2**20, transcendentals=0),
        name="shampoo_step",
    )(
        home, grad_parts.reshape(NB, B, H), left_stat, right_stat, left_root, right_root, first_moment, second_moment
    )


def solution(mesh):
    rows = P("dp", "mp", None)
    in_specs = (P("dp", None, "mp"), P(), rows, rows, rows, rows, rows, rows)
    out_specs = (rows, rows, rows, rows, P("dp", "mp"))
    return jax.shard_map(
        on_device, mesh=mesh, in_specs=in_specs, out_specs=out_specs, check_vma=False
    )
```

time: 296 us -> 60.7 us (0.21)
  waiting for transfers between devices: 119 us -> 0 us
  blocking collectives: 96 us -> 0 us
  Pallas kernels: 0 us -> 49.1 us
  matrix products: 31.8 us -> 0 us
  between operations: 14.2 us -> 0.66 us
  local copies, waits for them, and re-layouts: 21.7 us -> 10.6 us
  other arithmetic: 6.64 us -> 0 us
  starting transfers between devices: 5.96 us -> 0 us
    all_gather x2 -> x0, waiting for transfers between devices: 119 us -> none  [the longest x1 69.5 us: on_device(): shard_rows = lax.all_gather(slot_grads, 'mp', axis=1, tiled=True)]
    all_to_all x1 -> x0, blocking collectives: 63.3 us -> none  [on_device(): lax.all_to_all(ordered, ('dp', 'mp'), split_axis=0, concat_axis=0, tiled=...]
    pallas_call x0 -> x1, Pallas kernels: none -> 49.1 us  [on_device(): pl.pallas_call(kernel, out_shape=(rows_out,) * 4 + (jax.ShapeDtypeStruct(...]
    psum x1 -> x0, blocking collectives: 32.7 us -> none  [on_device(): norm_sums = lax.psum((adam_sums, precond_sums), 'mp')]
    dot_general x4 -> x0, matrix products: 31.8 us -> none  [the longest x1 10.9 us: on_device(): jnp.einsum('sik,sjk->sij', slot_grads, shard_rows, precision=HIGH)]
    gather x1 -> x0, local copies, waits for them, and re-layouts: 18.3 us -> none  [on_device(): jnp.take(partial_value, picked_rows, axis=0)]
    unnamed x11 -> x19, local copies, waits for them, and re-layouts: 0.73 us -> 10.6 us
    all_to_all x1 -> x0, starting transfers between devices: 5.88 us -> none  [on_device(): lax.all_to_all(strips_out, 'mp', split_axis=2, concat_axis=1, tiled=True)]
  transfers between devices with their start and end apart: 3 -> 0, of which waited for: 2 -> 0; matrix products, arithmetic and copies ran while one was open for 10% -> 0% of each run, Pallas kernels for 0% -> 0%
where the time goes in v1:
time: 60.7 us; the launch traced here: 60.3 us
  Pallas kernels  49.1 us (81%)
  local copies, waits for them, and re-layouts  10.6 us (17%)
  between operations  0.66 us (1%)
    pallas_call x1, Pallas kernels, on_device(): pl.pallas_call(kernel, out_shape=(rows_out,) * 4 + (jax.ShapeDtypeStruct(...  49.1 us
    unnamed x19, local copies, waits for them, and re-layouts  10.6 us

profile of v1, /device:TPU:1, one launch (start us, length us, event | category | flops | bytes accessed | tf_op | source)
XLA Modules:
  0.0 60.3 jit_solution(14208853033242746716)
XLA Ops:
  0.6 0.0 copy-start
  0.6 1.0 %copy-done = f32[8,32,512]{2,1,0:T(8,128)S(1)} copy-done((f32[8,32,512]{2,1,0:T(8,128)S(1)}, f32[8,32,512]{2,1,0:T(8,128)}, u32[]{:S(2)}) %copy-start) | copy-done | bytes 524312
  1.7 0.0 copy-start.1
  1.7 1.0 %copy-done.1 = f32[8,32,512]{2,1,0:T(8,128)S(1)} copy-done((f32[8,32,512]{2,1,0:T(8,128)S(1)}, f32[8,32,512]{2,1,0:T(8,128)}, u32[]{:S(2)}) %copy-start.1) | copy-done | bytes 524312
  2.7 0.0 copy-start.2
  2.7 1.0 %copy-done.2 = f32[8,32,512]{2,1,0:T(8,128)S(1)} copy-done((f32[8,32,512]{2,1,0:T(8,128)S(1)}, f32[8,32,512]{2,1,0:T(8,128)}, u32[]{:S(2)}) %copy-start.2) | copy-done | bytes 524312
  3.8 0.0 copy-start.3
  3.8 1.0 %copy-done.3 = f32[8,32,512]{2,1,0:T(8,128)S(1)} copy-done((f32[8,32,512]{2,1,0:T(8,128)S(1)}, f32[8,32,512]{2,1,0:T(8,128)}, u32[]{:S(2)}) %copy-start.3) | copy-done | bytes 524312
  4.8 0.0 copy-start.4
  4.8 0.9 %copy-done.4 = bf16[8,32,512]{2,1,0:T(8,128)(2,1)S(1)} copy-done((bf16[8,32,512]{2,1,0:T(8,128)(2,1)S(1)}, bf16[8,32,512]{2,1,0:T(8,128)(2,1)}, u32[]{:S(2)}) %copy-start.4) | copy-done | bytes 262168
  5.8 0.0 copy-start.5
  5.8 0.9 %copy-done.5 = bf16[8,32,512]{2,1,0:T(8,128)(2,1)S(1)} copy-done((bf16[8,32,512]{2,1,0:T(8,128)(2,1)S(1)}, bf16[8,32,512]{2,1,0:T(8,128)(2,1)}, u32[]{:S(2)}) %copy-start.5) | copy-done | bytes 262168
  6.7 0.0 copy-start.6
  6.7 0.7 %copy-done.6 = s32[8]{0:T(128)S(1)} copy-done((s32[8]{0:T(128)S(1)}, s32[8]{0:T(128)}, u32[]{:S(2)}) %copy-start.6) | copy-done | bytes 56
  7.4 49.1 %shampoo_step.1 = (f32[8,32,512]{2,1,0:T(8,128)S(1)}, f32[8,32,512]{2,1,0:T(8,128)S(1)}, f32[8,32,512]{2,1,0:T(8,128)S(1)}, f32[8,32,512]{2,1,0:T(8,128)S(1)}, bf16[512,256]{1,0:T(8,128)(2,1)S(1)}) custom-call(s32[8]{0:T(128)S(1)} %copy-done.6, f32[8,512,256]{2,1,0:T(8,128)} %bitcast.1, f32[8,32,512]{2,1,0:T(8,128)S(1)} %copy-done, ...), custom_call_target="tpu_custom_call" | custom-call | flops 2000000000 | bytes 9437184 | tf_op jit(solution)/shard_map/shampoo_step/pallas_call | solution.py:401
  56.4 0.8 %copy.18 = f32[8,32,512]{2,1,0:T(8,128)} copy(f32[8,32,512]{2,1,0:T(8,128)S(1)} %get-tuple-element.10) | data formatting | bytes 1048576
  57.2 0.8 %copy.19 = f32[8,32,512]{2,1,0:T(8,128)} copy(f32[8,32,512]{2,1,0:T(8,128)S(1)} %get-tuple-element.11) | data formatting | bytes 1048576
  58.0 0.8 %copy.20 = f32[8,32,512]{2,1,0:T(8,128)} copy(f32[8,32,512]{2,1,0:T(8,128)S(1)} %get-tuple-element.12) | data formatting | bytes 1048576
  58.8 0.8 %copy.21 = f32[8,32,512]{2,1,0:T(8,128)} copy(f32[8,32,512]{2,1,0:T(8,128)S(1)} %get-tuple-element.13) | data formatting | bytes 1048576
  59.6 0.7 %copy.22 = bf16[512,256]{1,0:T(8,128)(2,1)} copy(bf16[512,256]{1,0:T(8,128)(2,1)S(1)} %get-tuple-element.14) | data formatting | bytes 524288
Async XLA Ops:
  0.6 1.0 %copy-start = (f32[8,32,512]{2,1,0:T(8,128)S(1)}, f32[8,32,512]{2,1,0:T(8,128)}, u32[]{:S(2)}) copy-start(f32[8,32,512]{2,1,0:T(8,128)} %left_hbm.1) | copy-start | bytes 1572868
  1.7 1.0 %copy-start.1 = (f32[8,32,512]{2,1,0:T(8,128)S(1)}, f32[8,32,512]{2,1,0:T(8,128)}, u32[]{:S(2)}) copy-start(f32[8,32,512]{2,1,0:T(8,128)} %right_hbm.1) | copy-start | bytes 1572868
  2.7 1.0 %copy-start.2 = (f32[8,32,512]{2,1,0:T(8,128)S(1)}, f32[8,32,512]{2,1,0:T(8,128)}, u32[]{:S(2)}) copy-start(f32[8,32,512]{2,1,0:T(8,128)} %first_hbm.1) | copy-start | bytes 1572868
  3.8 1.0 %copy-start.3 = (f32[8,32,512]{2,1,0:T(8,128)S(1)}, f32[8,32,512]{2,1,0:T(8,128)}, u32[]{:S(2)}) copy-start(f32[8,32,512]{2,1,0:T(8,128)} %second_hbm.1) | copy-start | bytes 1572868
  4.8 0.9 %copy-start.4 = (bf16[8,32,512]{2,1,0:T(8,128)(2,1)S(1)}, bf16[8,32,512]{2,1,0:T(8,128)(2,1)}, u32[]{:S(2)}) copy-start(bf16[8,32,512]{2,1,0:T(8,128)(2,1)} %lroot_hbm.1) | copy-start | bytes 786436
  5.8 0.9 %copy-start.5 = (bf16[8,32,512]{2,1,0:T(8,128)(2,1)S(1)}, bf16[8,32,512]{2,1,0:T(8,128)(2,1)}, u32[]{:S(2)}) copy-start(bf16[8,32,512]{2,1,0:T(8,128)(2,1)} %rroot_hbm.1) | copy-start | bytes 786436
  6.7 0.7 %copy-start.6 = (s32[8]{0:T(128)S(1)}, s32[8]{0:T(128)}, u32[]{:S(2)}) copy-start(s32[8]{0:T(128)} %home.1) | copy-start | bytes 100

commit v2 on v1

--- a/solution.py
+++ b/solution.py
@@ -99,13 +99,13 @@
 
 def kernel(
     home, part_hbm, left_hbm, right_hbm, lroot_hbm, rroot_hbm, first_hbm, second_hbm,
-    new_left, new_right, new_first, new_second, update,
-    part, left, right, first, second, lroot, rroot,
+    new_left_hbm, new_right_hbm, new_first_hbm, new_second_hbm, update_hbm,
+    new_left, new_right, new_first, new_second, update, part, left, right, first, second, lroot, rroot,
     x1_out, x1_in, y1_out, y1_in, x2_out, x2_in, y2_out, y2_in,
     acc, ghigh, glow, grow_out, grow_in, prod_out, prod_in, pright, precond,
     sums_out, sums_in, pair_out, pair_in,
     load_sem, root_send, root_recv, x1_send, x1_recv, y1_send, y1_recv, s2_send, s2_recv,
-    core_send, core_recv, row_send, row_recv, sum_send, sum_recv,
+    core_send, core_recv, row_send, row_recv, sum_send, sum_recv, store_sem,
 ):
     d = lax.axis_index("dp")
     m = lax.axis_index("mp")
@@ -327,6 +327,17 @@
             adam = mean / (jnp.sqrt(square) + ADAM_EPS)
             total = total + fold(adam * adam)
         sums_out[i] = total
+    stores = [
+        pltpu.make_async_copy(src, dst, store_sem.at[i])
+        for i, (src, dst) in enumerate(
+            [
+                (new_first, new_first_hbm), (new_second, new_second_hbm), (new_left, new_left_hbm),
+                (new_right, new_right_hbm), (update, update_hbm),
+            ]
+        )
+    ]
+    stores[0].start()
+    stores[1].start()
     sum_copies = []
     for i, (a, b) in enumerate(PEERS):
         copy = remote(sums_out.at[i + 1], sums_in.at[i], sum_send.at[i], sum_recv.at[i], along_mp(-a, -b))
@@ -341,6 +352,7 @@
             for t, value in enumerate(decode_rows(prod_in.at[w, slot])):
                 cols = pl.ds(t * LANES, LANES)
                 new[slot, :, cols] = old[slot, :, cols] + value
+        stores[2 + w].start()
 
     total = sums_out[0]
     for i, copy in enumerate(sum_copies):
@@ -353,23 +365,37 @@
     norms = [jnp.sum(pair_out[w] + pair_in[w], axis=(0, 1), keepdims=True) for w in range(2)]
     graft = jnp.sqrt(norms[0]) / (jnp.sqrt(norms[1]) + NORM_EPS)
     update[...] = (pright[:, pl.ds(0, H)] * graft).astype(BF16)
+    stores[4].start()
 
     for copy in root_copies + row_copies + prod_copies + sum_copies:
         copy.wait_send()
     for copy in list(x1_copies.values()) + list(y1_copies.values()) + list(y2_copies.values()) + [x2_copy]:
         copy.wait_send()
+    for store in stores:
+        store.wait()
+
+
+def place(*refs):
+    sem = refs[-1]
+    n = len(refs) // 2
+    copies = [pltpu.make_async_copy(refs[i], refs[n + i], sem.at[i]) for i in range(n)]
+    for copy in copies:
+        copy.start()
+    for copy in copies:
+        copy.wait()
 
 
 def on_device(
     grad_parts, home, left_stat, right_stat, left_root, right_root, first_moment, second_moment
 ):
     in_hbm = pl.BlockSpec(memory_space=pltpu.HBM)
-    vmem = pl.BlockSpec(memory_space=pltpu.VMEM)
     n = len(PEERS)
     piece = (H + T, H)
     rows = (S * B // LANES + T, LANES)
     dma = pltpu.SemaphoreType.DMA
     scratch = [
+        *[pltpu.VMEM((NB, S, B), F32)] * 4,
+        pltpu.VMEM((B, H), BF16),
         pltpu.VMEM((NB, B, H), F32),
         *[pltpu.VMEM((NB, S, B), F32)] * 4,
         *[pltpu.VMEM((NB, 2, S, B), BF16)] * 2,
@@ -396,22 +422,33 @@
         *[dma((4,))] * 2,
         *[dma((3, n))] * 2,
         *[dma((n + 1,))] * 2,
+        dma((5,)),
     ]
     rows_out = jax.ShapeDtypeStruct((NB, S, B), F32)
-    return pl.pallas_call(
+    out_shape = (rows_out,) * 4 + (jax.ShapeDtypeStruct((B, H), BF16),)
+    made = pl.pallas_call(
         kernel,
-        out_shape=(rows_out,) * 4 + (jax.ShapeDtypeStruct((B, H), BF16),),
+        out_shape=out_shape,
         in_specs=[pl.BlockSpec(memory_space=pltpu.SMEM)] + [in_hbm] * 7,
-        out_specs=[vmem] * 5,
+        out_specs=[in_hbm] * 5,
         scratch_shapes=scratch,
         compiler_params=pltpu.CompilerParams(
-            collective_id=0, has_side_effects=True, vmem_limit_bytes=48 * 2**20
+            collective_id=0, has_side_effects=True, vmem_limit_bytes=58 * 2**20
         ),
         cost_estimate=pl.CostEstimate(flops=2 * 10**9, bytes_accessed=9 * 2**20, transcendentals=0),
         name="shampoo_step",
     )(
         home, grad_parts.reshape(NB, B, H), left_stat, right_stat, left_root, right_root, first_moment, second_moment
     )
+    return pl.pallas_call(
+        place,
+        out_shape=out_shape,
+        in_specs=[in_hbm] * 5,
+        out_specs=[in_hbm] * 5,
+        scratch_shapes=[dma((5,))],
+        compiler_params=pltpu.CompilerParams(vmem_limit_bytes=58 * 2**20),
+        name="place_outputs",
+    )(*made)
 
 
 def solution(mesh):

time: 60.7 us -> 124 us (2.04)
  Pallas kernels: 49.1 us -> 123 us
  local copies, waits for them, and re-layouts: 10.6 us -> 0 us
    pallas_call x1 -> x2, Pallas kernels: 49.1 us -> 123 us  [the longest x1 72.6 us: on_device(): pl.pallas_call(place, out_shape=out_shape, in_specs=[in_hbm] * 5, out_spe...]
    unnamed x19 -> x0, local copies, waits for them, and re-layouts: 10.6 us -> none
where the time goes in v2:
time: 124 us; the launch traced here: 123 us
  Pallas kernels  123 us (99%)
    pallas_call x1, Pallas kernels, on_device(): pl.pallas_call(place, out_shape=out_shape, in_specs=[in_hbm] * 5, out_spe...  72.6 us
    pallas_call x1, Pallas kernels, on_device(): pl.pallas_call(kernel, out_shape=out_shape, in_specs=[pl.BlockSpec(memory...  50.2 us

profile of v2, /device:TPU:1, one launch (start us, length us, event | category | flops | bytes accessed | tf_op | source)
XLA Modules:
  0.0 123.4 jit_solution(4043427237318534639)
XLA Ops:
  0.6 50.2 %shampoo_step.1 = (f32[8,32,512]{2,1,0:T(8,128)}, f32[8,32,512]{2,1,0:T(8,128)}, f32[8,32,512]{2,1,0:T(8,128)}, f32[8,32,512]{2,1,0:T(8,128)}, bf16[512,256]{1,0:T(8,128)(2,1)}) custom-call(s32[8]{0:T(128)} %home.1, f32[8,512,256]{2,1,0:T(8,128)} %bitcast.1, f32[8,32,512]{2,1,0:T(8,128)} %left_hbm.1, f32[8,32,512]{2,1,0:T(8,128)} %right_hbm.1, ...), custom_call_target="tpu_custom_call" | custom-call | flops 2000000000 | bytes 9437184 | tf_op jit(solution)/shard_map/shampoo_step/pallas_call | solution.py:429
  50.8 72.6 %place_outputs.1 = (f32[8,32,512]{2,1,0:T(8,128)}, f32[8,32,512]{2,1,0:T(8,128)}, f32[8,32,512]{2,1,0:T(8,128)}, f32[8,32,512]{2,1,0:T(8,128)}, bf16[512,256]{1,0:T(8,128)(2,1)}) custom-call(f32[8,32,512]{2,1,0:T(8,128)} %get-tuple-element.10.refs_0_, f32[8,32,512]{2,1,0:T(8,128)} %get-tuple-element.11.refs_1_, f32[8,32,512]{2,1,0:T(8,128)} %get-tuple-element.12.refs_2_, ...), custom_call_target="tpu_custom_call" | custom-call | tf_op jit(solution)/shard_map/place_outputs/pallas_call | solution.py:443

commit v3 on v1

v3 whole, which is shorter than its diff:
```python
import functools
import math

import jax
import jax.numpy as jnp
from jax import lax
from jax.experimental import pallas as pl
from jax.experimental.pallas import tpu as pltpu
from jax.sharding import PartitionSpec as P

FIRST_DECAY = 0.9
SECOND_DECAY = 0.999
ADAM_EPS = 1e-08
NORM_EPS = 1e-06
MESH = pl.DeviceIdType.MESH
F32 = jnp.float32
BF16 = jnp.bfloat16
I16 = jnp.int16
I32 = jnp.int32

B = 512
H = 256
XROWS = 192
YROWS = B - XROWS
S = 32
T = 16
STRIDE = 64
LANES = 128
WIDE = B // LANES * S
NB = 8
NY = 4
FULL = 32760.0
STEP = math.log(2.0) / 4.0
TINY = 1e-30

PEERS = [(a, b) for a in range(2) for b in range(4) if (a, b) != (0, 0)]


def code_of(peak):
    return jnp.ceil(jnp.log(jnp.maximum(peak, TINY)) * (1.0 / STEP))


def coded(x):
    return jnp.floor(x + 0.5).astype(I32).astype(I16)


def scale_of(code):
    return jnp.exp(code.astype(I32).astype(F32) * STEP) * (1.0 / FULL)


def decoded(values, scale):
    return values.astype(I32).astype(F32) * scale


def encode_piece(n, read, out, keep=None):
    tiles = range(H // LANES)

    def look(i, peak):
        r = pl.multiple_of(i * STRIDE, STRIDE)
        for t in tiles:
            x = read(t, r)
            if keep is not None:
                keep[pl.ds(r, STRIDE), pl.ds(t * LANES, LANES)] = x
            peak = jnp.maximum(peak, jnp.max(jnp.abs(x).reshape(STRIDE // T, T, LANES), axis=0))
        return peak

    code = code_of(lax.fori_loop(0, n // STRIDE, look, jnp.zeros((T, LANES), F32)))
    factor = jnp.exp(code * -STEP) * FULL

    def write(i, carry):
        r = pl.multiple_of(i * STRIDE, STRIDE)
        for t in tiles:
            x = read(t, r) if keep is None else keep[pl.ds(r, STRIDE), pl.ds(t * LANES, LANES)]
            x = x.reshape(STRIDE // T, T, LANES) * factor[None]
            out[pl.ds(t * n + r, STRIDE), :] = coded(x).reshape(STRIDE, LANES)
        return carry

    lax.fori_loop(0, n // STRIDE, write, 0)
    out[pl.ds(H // LANES * n, T), :] = code.astype(I32).astype(I16)


def sum_of(n, own, arrived):
    scales = [scale_of(ref[pl.ds(H // LANES * n, T), :])[None] for ref in arrived]

    def read(t, r):
        x = own(t, r)
        for ref, scale in zip(arrived, scales):
            values = ref[pl.ds(t * n + r, STRIDE), :].reshape(STRIDE // T, T, LANES)
            x = x + decoded(values, scale).reshape(STRIDE, LANES)
        return x

    return read


def encode_rows(x, group, out, first):
    n = B // LANES
    parts = [x[:, t * LANES : (t + 1) * LANES].reshape(S // group, group, LANES) for t in range(n)]
    code = code_of(functools.reduce(jnp.maximum, [jnp.max(jnp.abs(p), axis=0) for p in parts]))
    factor = jnp.exp(code * -STEP) * FULL
    for t in range(n):
        out[pl.ds(first + t * S, S), :] = coded(parts[t] * factor[None]).reshape(S, LANES)
    return code


def decode_rows(codes, first, scale):
    group = scale.shape[0]
    return [
        decoded(codes[pl.ds(first + t * S, S), :].reshape(S // group, group, LANES), scale[None]).reshape(S, LANES)
        for t in range(B // LANES)
    ]


def dot(a, b, dims=((1,), (0,))):
    return lax.dot_general(a, b, (dims, ((), ())), preferred_element_type=F32)


def split(x):
    high = x.astype(BF16)
    return high, (x - high.astype(F32)).astype(BF16)


def fold(x):
    r, c = x.shape
    x = jnp.sum(x.reshape(r // 8, 8, c), axis=0)
    return functools.reduce(jnp.add, [x[:, t * LANES : (t + 1) * LANES] for t in range(c // LANES)])


def kernel(
    home_hbm, part_hbm, lroot_hbm, rroot_hbm, first_hbm, second_hbm,
    prod_in, new_first_hbm, new_second_hbm, update_hbm,
    home, part, first, second, new_first, new_second, update, lroot, rroot,
    x1_out, x1_in, y1_out, y1_in, x2_out, x2_in, y2_out, y2_in,
    work, ghigh, glow, grow_out, grow_in, prod_out, left_codes, pleft, pright,
    sums_out, sums_in, pair_out, pair_in,
    load_sem, root_send, root_recv, x1_send, x1_recv, y1_send, y1_recv, s2_send, s2_recv,
    core_send, core_recv, row_send, row_recv, sum_send, sum_recv, store_sem,
):
    d = lax.axis_index("dp")
    m = lax.axis_index("mp")
    xl, y = d // NY, d % NY
    xh, z, k = m // 8, (m // 2) % 4, m % 2
    c = m // 2

    partner = (d, m + 1 - 2 * k)
    across = ((1 - xl) * NY + y, m)

    def along_y(j):
        return (xl * NY + (y + j) % NY, m)

    def chip_at(a, b):
        return ((xh + a) % 2) * 4 + (z + b) % 4

    def along_mp(a, b):
        return (d, chip_at(a, b) * 2 + k)

    def remote(src, dst, send, recv, device):
        return pltpu.make_async_remote_copy(
            src_ref=src, dst_ref=dst, send_sem=send, recv_sem=recv, device_id=device, device_id_type=MESH
        )

    loads = [
        pltpu.make_async_copy(src, dst, load_sem.at[i])
        for i, (src, dst) in enumerate(
            [
                (home_hbm, home), (part_hbm, part), (first_hbm, first), (second_hbm, second),
                (lroot_hbm.at[c], lroot.at[c, k]), (rroot_hbm.at[c], rroot.at[c, k]),
            ]
        )
    ]
    loads[0].start()
    loads[1].start()

    barrier = pltpu.get_barrier_semaphore()
    greeted = [partner, across] + [along_y(j) for j in (1, 2, 3)] + [along_mp(a, b) for a, b in PEERS]
    for device in greeted:
        pl.semaphore_signal(barrier, inc=1, device_id=device, device_id_type=MESH)
    pl.semaphore_wait(barrier, len(greeted))

    root_copies = []
    for i, (a, b) in enumerate(PEERS):
        there = chip_at(a, b)
        for w, (src, dst) in enumerate(((lroot_hbm, lroot), (rroot_hbm, rroot))):
            copy = remote(src.at[there], dst.at[c, k], root_send.at[w, i], root_recv.at[w, i], along_mp(a, b))
            copy.start()
            root_copies.append(copy)
    for load in loads[2:]:
        load.start()

    def source(q):
        return functools.reduce(jnp.maximum, [jnp.where(home[r] == q, r, 0) for r in range(NB)])

    def own_piece(to_x, j, start):
        row = source(to_x * NY + (y + j) % NY)
        return lambda t, r: part[row, pl.ds(start + r, STRIDE), pl.ds(t * LANES, LANES)]

    loads[0].wait()
    loads[1].wait()
    x1_copies, y1_copies = {}, {}

    def send_x1(j):
        encode_piece(XROWS, own_piece(1 - xl, j, YROWS), x1_out.at[j])
        x1_copies[j] = remote(x1_out.at[j], x1_in.at[j], x1_send.at[j], x1_recv.at[j], across)
        x1_copies[j].start()

    def send_y1(w, j):
        n = w * 3 + j - 1
        encode_piece(YROWS, own_piece(1 - xl if w == 0 else xl, j, 0), y1_out.at[n])
        y1_copies[w, j] = remote(y1_out.at[n], y1_in.at[n], y1_send.at[n], y1_recv.at[n], along_y(j))
        y1_copies[w, j].start()

    for j in (1, 3, 2):
        send_y1(0, j)
        send_x1(j)
    for j in (1, 3, 2):
        send_y1(1, j)
    send_x1(0)

    y2_copies = {}
    for j in (1, 3, 2):
        x1_copies[j].wait_recv()
        read = sum_of(XROWS, own_piece(xl, j, YROWS), [x1_in.at[j]])
        encode_piece(XROWS, read, y2_out.at[j - 1], work)
        y2_copies[j] = remote(y2_out.at[j - 1], y2_in.at[j - 1], s2_send.at[j], s2_recv.at[j], along_y(j))
        y2_copies[j].start()

    for j in (1, 2, 3):
        y1_copies[0, j].wait_recv()
    read = sum_of(YROWS, own_piece(1 - xl, 0, 0), [y1_in.at[n] for n in range(3)])
    encode_piece(YROWS, read, x2_out, work)
    x2_copy = remote(x2_out, x2_in, s2_send.at[0], s2_recv.at[0], across)
    x2_copy.start()

    for copy in root_copies:
        copy.wait_recv()
    loads[4].wait()
    loads[5].wait()
    core_copies = []
    for w, ref in enumerate((lroot, rroot)):
        copy = remote(ref.at[:, k], ref.at[:, k], core_send.at[w], core_recv.at[w], partner)
        copy.start()
        core_copies.append(copy)

    strip = pl.ds(pl.multiple_of(k * H, H), H)
    block_copies = []

    def finish(n, start, read, w):
        def step(i, carry):
            r = pl.multiple_of(i * STRIDE, STRIDE)
            for t in range(H // LANES):
                mine = pl.ds(pl.multiple_of(k * H + t * LANES, LANES), LANES)
                high, low = split(read(t, r))
                ghigh[pl.ds(start + r, STRIDE), mine] = high
                glow[pl.ds(start + r, STRIDE), mine] = low
            return carry

        lax.fori_loop(0, n // STRIDE, step, 0)
        for i, ref in enumerate((ghigh, glow)):
            here = ref.at[pl.ds(start, n), strip]
            copy = remote(here, here, core_send.at[2 + 2 * w + i], core_recv.at[2 + 2 * w + i], partner)
            copy.start()
            block_copies.append(copy)

    x1_copies[0].wait_recv()
    for j in (1, 3, 2):
        y2_copies[j].wait_recv()
    arrived = [x1_in.at[0]] + [y2_in.at[n] for n in range(3)]
    finish(XROWS, YROWS, sum_of(XROWS, own_piece(xl, 0, YROWS), arrived), 0)
    for j in (1, 2, 3):
        y1_copies[1, j].wait_recv()
    x2_copy.wait_recv()
    arrived = [y1_in.at[n] for n in range(3, 6)] + [x2_in]
    finish(YROWS, 0, sum_of(YROWS, own_piece(xl, 0, 0), arrived), 1)

    for copy in block_copies:
        copy.wait_recv()

    def rows_for(there):
        return pl.ds(pl.multiple_of(there * 2 * S + k * S, S), S)

    row_copies = []
    for i, (a, b) in enumerate(PEERS + [(0, 0)]):
        rows = rows_for(chip_at(a, b))
        value = ghigh[rows, :].astype(F32) + glow[rows, :].astype(F32)
        out = grow_out.at[i] if a or b else grow_in.at[c]
        out[pl.ds(WIDE, T), :] = encode_rows(value, T, out, 0).astype(I32).astype(I16)
        if a or b:
            copy = remote(out, grow_in.at[c], row_send.at[0, i], row_recv.at[0, i], along_mp(a, b))
            copy.start()
            row_copies.append(copy)

    high_rows = jnp.concatenate([ghigh[rows_for(t), :] for t in range(NB)], axis=0)
    low_rows = jnp.concatenate([glow[rows_for(t), :] for t in range(NB)], axis=0)
    nt = ((1,), (1,))
    pleft[...] = dot(high_rows, ghigh[...], nt) + (dot(high_rows, glow[...], nt) + dot(low_rows, ghigh[...], nt))
    prod_copies = []

    def send_products(w, i, first, size):
        a, b = (PEERS + [(0, 0)])[i]
        here, there = prod_out.at[i, pl.ds(first, size)], prod_in.at[c, pl.ds(first, size)]
        if a or b:
            copy = remote(here, there, row_send.at[1 + w, i], row_recv.at[1 + w, i], along_mp(a, b))
            prod_copies.append(copy)
        else:
            copy = pltpu.make_async_copy(here, there, store_sem.at[3 + w])
            stores.append(copy)
        copy.start()

    stores = []
    for i, (a, b) in enumerate(PEERS + [(0, 0)]):
        value = pleft[pl.ds(pl.multiple_of(chip_at(a, b) * S, S), S), :]
        left_codes[i] = encode_rows(value, T // 2, prod_out.at[i], 0)
        send_products(0, i, 0, WIDE)
    tn = ((0,), (0,))
    pright[...] = dot(ghigh[...], ghigh[...], tn) + (
        dot(ghigh[...], glow[...], tn) + dot(glow[...], ghigh[...], tn)
    )
    for i, (a, b) in enumerate(PEERS + [(0, 0)]):
        code = encode_rows(pright[rows_for(chip_at(a, b)), :], T // 2, prod_out.at[i], WIDE)
        codes = jnp.concatenate([left_codes[i], code], axis=0)
        prod_out[i, pl.ds(2 * WIDE, T), :] = codes.astype(I32).astype(I16)
        send_products(1, i, WIDE, WIDE + T)

    for copy in core_copies:
        copy.wait_recv()
    rcols = jnp.concatenate([rroot[a, b, :, strip] for a in range(NB) for b in range(2)], axis=0)
    inner = dot(ghigh[...], rcols) + dot(glow[...], rcols)
    inner_high, inner_low = split(inner)
    lrows = lroot[...].reshape(B, B)
    applied = dot(lrows, inner_high) + dot(lrows, inner_low)
    pright[:, pl.ds(0, H)] = applied
    pair_out[1] = fold(applied * applied)

    loads[2].wait()
    loads[3].wait()
    sum_copies = []
    for i, (a, b) in enumerate(PEERS + [(0, 0)]):
        slot = chip_at(-a, -b)
        if a or b:
            row_copies[i].wait_recv()
        total = jnp.zeros((8, LANES), F32)
        scale = scale_of(grow_in[slot, pl.ds(WIDE, T), :])
        for t, grad in enumerate(decode_rows(grow_in.at[slot], 0, scale)):
            cols = pl.ds(t * LANES, LANES)
            mean = FIRST_DECAY * first[slot, :, cols] + (1.0 - FIRST_DECAY) * grad
            square = SECOND_DECAY * second[slot, :, cols] + (1.0 - SECOND_DECAY) * grad * grad
            new_first[slot, :, cols] = mean
            new_second[slot, :, cols] = square
            adam = mean / (jnp.sqrt(square) + ADAM_EPS)
            total = total + fold(adam * adam)
        sums_out[i] = total
        if a or b:
            copy = remote(sums_out.at[i], sums_in.at[i], sum_send.at[i], sum_recv.at[i], along_mp(-a, -b))
            copy.start()
            sum_copies.append(copy)
    moment_stores = [
        pltpu.make_async_copy(new_first, new_first_hbm, store_sem.at[0]),
        pltpu.make_async_copy(new_second, new_second_hbm, store_sem.at[1]),
    ]
    for store in moment_stores:
        store.start()

    total = sums_out[len(PEERS)]
    for i, copy in enumerate(sum_copies):
        copy.wait_recv()
        total = total + sums_in[i]
    pair_out[0] = total
    pair_copy = remote(pair_out, pair_in, sum_send.at[len(PEERS)], sum_recv.at[len(PEERS)], partner)
    pair_copy.start()
    pair_copy.wait_recv()
    norms = [jnp.sum(pair_out[w] + pair_in[w], axis=(0, 1), keepdims=True) for w in range(2)]
    graft = jnp.sqrt(norms[0]) / (jnp.sqrt(norms[1]) + NORM_EPS)
    update[...] = (pright[:, pl.ds(0, H)] * graft).astype(BF16)
    update_store = pltpu.make_async_copy(update, update_hbm, store_sem.at[2])
    update_store.start()

    for copy in prod_copies:
        copy.wait_recv()
    sent = [x2_copy, pair_copy] + root_copies + core_copies + block_copies + row_copies + prod_copies + sum_copies
    for copy in sent + list(x1_copies.values()) + list(y1_copies.values()) + list(y2_copies.values()):
        copy.wait_send()
    for store in stores + moment_stores + [update_store]:
        store.wait()


def finish_kernel(
    prod_hbm, left_hbm, right_hbm, made_first, made_second, made_update,
    left_out, right_out, first_out, second_out, update_out,
    prod, left, right, first, second, update, load_sem, store_sem,
):
    through = [(made_first, first, first_out), (made_second, second, second_out), (made_update, update, update_out)]
    stats = [(left_hbm, left, left_out), (right_hbm, right, right_out)]
    loads = [pltpu.make_async_copy(prod_hbm, prod, load_sem.at[0])]
    for i, (src, dst, _) in enumerate(stats + through):
        loads.append(pltpu.make_async_copy(src, dst, load_sem.at[1 + i]))
    stores = [pltpu.make_async_copy(src, dst, store_sem.at[i]) for i, (_, src, dst) in enumerate(stats + through)]
    for load in loads:
        load.start()
    loads[0].wait()
    for w, ref in enumerate((left, right)):
        loads[1 + w].wait()

        def add(slot, carry):
            code = prod[slot, pl.ds(2 * WIDE, T), :].astype(F32)[w * (T // 2) : (w + 1) * (T // 2)]
            for t, value in enumerate(decode_rows(prod.at[slot], w * WIDE, jnp.exp(code * STEP) * (1.0 / FULL))):
                ref[slot, :, pl.ds(t * LANES, LANES)] += value
            return carry

        lax.fori_loop(0, NB, add, 0)
        stores[w].start()
    for i in range(len(through)):
        loads[3 + i].wait()
        stores[2 + i].start()
    for store in stores:
        store.wait()


def on_device(
    grad_parts, home, left_stat, right_stat, left_root, right_root, first_moment, second_moment
):
    in_hbm = pl.BlockSpec(memory_space=pltpu.HBM)
    n = len(PEERS)
    xpiece = (H // LANES * XROWS + T, LANES)
    ypiece = (H // LANES * YROWS + T, LANES)
    rows = (WIDE + T, LANES)
    products = (2 * WIDE + T, LANES)
    stat = pltpu.VMEM((NB, S, B), F32)
    tile = pltpu.VMEM((B, H), BF16)
    dma = pltpu.SemaphoreType.DMA
    scratch = [
        pltpu.SMEM((NB,), I32),
        pltpu.VMEM((NB, B, H), F32),
        *[stat] * 4,
        tile,
        *[pltpu.VMEM((NB, 2, S, B), BF16)] * 2,
        *[pltpu.VMEM((4, *xpiece), I16)] * 2,
        *[pltpu.VMEM((6, *ypiece), I16)] * 2,
        *[pltpu.VMEM(ypiece, I16)] * 2,
        *[pltpu.VMEM((3, *xpiece), I16)] * 2,
        pltpu.VMEM((B, H), F32),
        *[pltpu.VMEM((B, B), BF16)] * 2,
        pltpu.VMEM((n, *rows), I16),
        pltpu.VMEM((NB, *rows), I16),
        pltpu.VMEM((NB, *products), I16),
        pltpu.VMEM((NB, T // 2, LANES), F32),
        pltpu.VMEM((H, B), F32),
        pltpu.VMEM((B, B), F32),
        pltpu.VMEM((NB, 8, LANES), F32),
        pltpu.VMEM((n, 8, LANES), F32),
        *[pltpu.VMEM((2, 8, LANES), F32)] * 2,
        dma((6,)),
        *[dma((2, n))] * 2,
        *[dma((4,))] * 2,
        *[dma((6,))] * 2,
        *[dma((4,))] * 2,
        *[dma((6,))] * 2,
        *[dma((3, n))] * 2,
        *[dma((n + 1,))] * 2,
        dma((5,)),
    ]
    stat_out = jax.ShapeDtypeStruct((NB, S, B), F32)
    tile_out = jax.ShapeDtypeStruct((B, H), BF16)
    made = pl.pallas_call(
        kernel,
        out_shape=(jax.ShapeDtypeStruct((NB, *products), I16), stat_out, stat_out, tile_out),
        in_specs=[in_hbm] * 6,
        out_specs=[in_hbm] * 4,
        scratch_shapes=scratch,
        compiler_params=pltpu.CompilerParams(
            collective_id=0, has_side_effects=True, vmem_limit_bytes=58 * 2**20
        ),
        cost_estimate=pl.CostEstimate(flops=2 * 10**9, bytes_accessed=9 * 2**20, transcendentals=0),
        name="shampoo_step",
    )(home, grad_parts.reshape(NB, B, H), left_root, right_root, first_moment, second_moment)
    return pl.pallas_call(
        finish_kernel,
        out_shape=(stat_out,) * 4 + (tile_out,),
        in_specs=[in_hbm] * 6,
        out_specs=[in_hbm] * 5,
        scratch_shapes=[pltpu.VMEM((NB, *products), I16), *[stat] * 4, tile, dma((6,)), dma((5,))],
        compiler_params=pltpu.CompilerParams(vmem_limit_bytes=58 * 2**20),
        name="finish_outputs",
    )(made[0], left_stat, right_stat, *made[1:])


def solution(mesh):
    rows = P("dp", "mp", None)
    in_specs = (P("dp", None, "mp"), P(), rows, rows, rows, rows, rows, rows)
    out_specs = (rows, rows, rows, rows, P("dp", "mp"))
    return jax.shard_map(
        on_device, mesh=mesh, in_specs=in_specs, out_specs=out_specs, check_vma=False
    )
```

time: 60.7 us -> 51.1 us (0.84)
  local copies, waits for them, and re-layouts: 10.6 us -> 0 us
  Pallas kernels: 49.1 us -> 50.3 us
    unnamed x19 -> x0, local copies, waits for them, and re-layouts: 10.6 us -> none
    pallas_call x1 -> x2, Pallas kernels: 49.1 us -> 50.3 us  [the longest x1 47.5 us: on_device(): pl.pallas_call(kernel, out_shape=(jax.ShapeDtypeStruct((NB, *products), I...]
where the time goes in v3:
time: 51.1 us; the launch traced here: 51 us
  Pallas kernels  50.3 us (98%)
  between operations  0.64 us (1%)
    pallas_call x1, Pallas kernels, on_device(): pl.pallas_call(kernel, out_shape=(jax.ShapeDtypeStruct((NB, *products), I...  47.5 us
    pallas_call x1, Pallas kernels, on_device(): pl.pallas_call(finish_kernel, out_shape=(stat_out,) * 4 + (tile_out,), in...  2.85 us

profile of v3, /device:TPU:1, one launch (start us, length us, event | category | flops | bytes accessed | tf_op | source)
XLA Modules:
  0.0 51.0 jit_solution(8327163492668064652)
XLA Ops:
  0.6 47.5 %shampoo_step.1 = (s16[8,272,128]{2,1,0:T(8,128)(2,1)}, f32[8,32,512]{2,1,0:T(8,128)}, f32[8,32,512]{2,1,0:T(8,128)}, bf16[512,256]{1,0:T(8,128)(2,1)}) custom-call(s32[8]{0:T(128)} %home_hbm.1, f32[8,512,256]{2,1,0:T(8,128)} %bitcast.1, bf16[8,32,512]{2,1,0:T(8,128)(2,1)} %lroot_hbm.1, bf16[8,32,512]{2,1,0:T(8,128)(2,1)} %rroot_hbm.1, ...), custom_call_target="tpu_custom_call" | custom-call | flops 2000000000 | bytes 9437184 | tf_op jit(solution)/shard_map/shampoo_step/pallas_call | solution.py:462
  48.1 2.9 %finish_outputs.1 = (f32[8,32,512]{2,1,0:T(8,128)}, f32[8,32,512]{2,1,0:T(8,128)}, f32[8,32,512]{2,1,0:T(8,128)}, f32[8,32,512]{2,1,0:T(8,128)}, bf16[512,256]{1,0:T(8,128)(2,1)}) custom-call(s16[8,272,128]{2,1,0:T(8,128)(2,1)} %get-tuple-element.9.prod_hbm, f32[8,32,512]{2,1,0:T(8,128)} %left_hbm.1, f32[8,32,512]{2,1,0:T(8,128)} %right_hbm.1, ...), custom_call_target="tpu_custom_call" | custom-call | tf_op jit(solution)/shard_map/finish_outputs/pallas_call | solution.py:474

commit v4 on v3

--- a/solution.py
+++ b/solution.py
@@ -33,7 +33,7 @@
 STEP = math.log(2.0) / 4.0
 TINY = 1e-30
 
-PEERS = [(a, b) for a in range(2) for b in range(4) if (a, b) != (0, 0)]
+PEERS = [(1, 2), (1, 1), (1, 3), (0, 2), (1, 0), (0, 1), (0, 3)]
 
 
 def code_of(peak):
@@ -318,17 +318,6 @@
         code = encode_rows(pright[rows_for(chip_at(a, b)), :], T // 2, prod_out.at[i], WIDE)
         codes = jnp.concatenate([left_codes[i], code], axis=0)
         prod_out[i, pl.ds(2 * WIDE, T), :] = codes.astype(I32).astype(I16)
-        send_products(1, i, WIDE, WIDE + T)
-
-    for copy in core_copies:
-        copy.wait_recv()
-    rcols = jnp.concatenate([rroot[a, b, :, strip] for a in range(NB) for b in range(2)], axis=0)
-    inner = dot(ghigh[...], rcols) + dot(glow[...], rcols)
-    inner_high, inner_low = split(inner)
-    lrows = lroot[...].reshape(B, B)
-    applied = dot(lrows, inner_high) + dot(lrows, inner_low)
-    pright[:, pl.ds(0, H)] = applied
-    pair_out[1] = fold(applied * applied)
 
     loads[2].wait()
     loads[3].wait()
@@ -352,6 +341,19 @@
             copy = remote(sums_out.at[i], sums_in.at[i], sum_send.at[i], sum_recv.at[i], along_mp(-a, -b))
             copy.start()
             sum_copies.append(copy)
+    for i in range(NB):
+        send_products(1, i, WIDE, WIDE + T)
+
+    for copy in core_copies:
+        copy.wait_recv()
+    rcols = jnp.concatenate([rroot[a, b, :, strip] for a in range(NB) for b in range(2)], axis=0)
+    inner = dot(ghigh[...], rcols) + dot(glow[...], rcols)
+    inner_high, inner_low = split(inner)
+    lrows = lroot[...].reshape(B, B)
+    applied = dot(lrows, inner_high) + dot(lrows, inner_low)
+    pright[:, pl.ds(0, H)] = applied
+    pair_out[1] = fold(applied * applied)
+
     moment_stores = [
         pltpu.make_async_copy(new_first, new_first_hbm, store_sem.at[0]),
         pltpu.make_async_copy(new_second, new_second_hbm, store_sem.at[1]),

time: 51.1 us -> 49.4 us (0.967)
  Pallas kernels: 50.3 us -> 48.6 us
    pallas_call x1, Pallas kernels: 47.5 us -> 45.8 us  [on_device(): pl.pallas_call(kernel, out_shape=(jax.ShapeDtypeStruct((NB, *products), I...]
where the time goes in v4:
time: 49.4 us; the launch traced here: 49.3 us
  Pallas kernels  48.6 us (98%)
  between operations  0.64 us (1%)
    pallas_call x1, Pallas kernels, on_device(): pl.pallas_call(kernel, out_shape=(jax.ShapeDtypeStruct((NB, *products), I...  45.8 us
    pallas_call x1, Pallas kernels, on_device(): pl.pallas_call(finish_kernel, out_shape=(stat_out,) * 4 + (tile_out,), in...  2.85 us

profile of v4, /device:TPU:1, one launch (start us, length us, event | category | flops | bytes accessed | tf_op | source)
XLA Modules:
  0.0 49.3 jit_solution(1997821207596990121)
XLA Ops:
  0.6 45.8 %shampoo_step.1 = (s16[8,272,128]{2,1,0:T(8,128)(2,1)}, f32[8,32,512]{2,1,0:T(8,128)}, f32[8,32,512]{2,1,0:T(8,128)}, bf16[512,256]{1,0:T(8,128)(2,1)}) custom-call(s32[8]{0:T(128)} %home_hbm.1, f32[8,512,256]{2,1,0:T(8,128)} %bitcast.1, bf16[8,32,512]{2,1,0:T(8,128)(2,1)} %lroot_hbm.1, bf16[8,32,512]{2,1,0:T(8,128)(2,1)} %rroot_hbm.1, ...), custom_call_target="tpu_custom_call" | custom-call | flops 2000000000 | bytes 9437184 | tf_op jit(solution)/shard_map/shampoo_step/pallas_call | solution.py:464
  46.4 2.9 %finish_outputs.1 = (f32[8,32,512]{2,1,0:T(8,128)}, f32[8,32,512]{2,1,0:T(8,128)}, f32[8,32,512]{2,1,0:T(8,128)}, f32[8,32,512]{2,1,0:T(8,128)}, bf16[512,256]{1,0:T(8,128)(2,1)}) custom-call(s16[8,272,128]{2,1,0:T(8,128)(2,1)} %get-tuple-element.9.prod_hbm, f32[8,32,512]{2,1,0:T(8,128)} %left_hbm.1, f32[8,32,512]{2,1,0:T(8,128)} %right_hbm.1, ...), custom_call_target="tpu_custom_call" | custom-call | tf_op jit(solution)/shard_map/finish_outputs/pallas_call | solution.py:476

commit v5 on v4

--- a/solution.py
+++ b/solution.py
@@ -127,8 +127,8 @@
 
 def kernel(
     home_hbm, part_hbm, lroot_hbm, rroot_hbm, first_hbm, second_hbm,
-    prod_in, new_first_hbm, new_second_hbm, update_hbm,
-    home, part, first, second, new_first, new_second, update, lroot, rroot,
+    prod_in, new_first, new_second, update,
+    home, part, first, second, lroot, rroot,
     x1_out, x1_in, y1_out, y1_in, x2_out, x2_in, y2_out, y2_in,
     work, ghigh, glow, grow_out, grow_in, prod_out, left_codes, pleft, pright,
     sums_out, sums_in, pair_out, pair_in,
@@ -301,7 +301,7 @@
             copy = remote(here, there, row_send.at[1 + w, i], row_recv.at[1 + w, i], along_mp(a, b))
             prod_copies.append(copy)
         else:
-            copy = pltpu.make_async_copy(here, there, store_sem.at[3 + w])
+            copy = pltpu.make_async_copy(here, there, store_sem.at[w])
             stores.append(copy)
         copy.start()
 
@@ -354,13 +354,6 @@
     pright[:, pl.ds(0, H)] = applied
     pair_out[1] = fold(applied * applied)
 
-    moment_stores = [
-        pltpu.make_async_copy(new_first, new_first_hbm, store_sem.at[0]),
-        pltpu.make_async_copy(new_second, new_second_hbm, store_sem.at[1]),
-    ]
-    for store in moment_stores:
-        store.start()
-
     total = sums_out[len(PEERS)]
     for i, copy in enumerate(sum_copies):
         copy.wait_recv()
@@ -372,46 +365,38 @@
     norms = [jnp.sum(pair_out[w] + pair_in[w], axis=(0, 1), keepdims=True) for w in range(2)]
     graft = jnp.sqrt(norms[0]) / (jnp.sqrt(norms[1]) + NORM_EPS)
     update[...] = (pright[:, pl.ds(0, H)] * graft).astype(BF16)
-    update_store = pltpu.make_async_copy(update, update_hbm, store_sem.at[2])
-    update_store.start()
 
     for copy in prod_copies:
         copy.wait_recv()
     sent = [x2_copy, pair_copy] + root_copies + core_copies + block_copies + row_copies + prod_copies + sum_copies
     for copy in sent + list(x1_copies.values()) + list(y1_copies.values()) + list(y2_copies.values()):
         copy.wait_send()
-    for store in stores + moment_stores + [update_store]:
+    for store in stores:
         store.wait()
 
 
 def finish_kernel(
-    prod_hbm, left_hbm, right_hbm, made_first, made_second, made_update,
+    prod, left, right, first, second, update,
     left_out, right_out, first_out, second_out, update_out,
-    prod, left, right, first, second, update, load_sem, store_sem,
+    new_left, new_right, sem,
 ):
-    through = [(made_first, first, first_out), (made_second, second, second_out), (made_update, update, update_out)]
-    stats = [(left_hbm, left, left_out), (right_hbm, right, right_out)]
-    loads = [pltpu.make_async_copy(prod_hbm, prod, load_sem.at[0])]
-    for i, (src, dst, _) in enumerate(stats + through):
-        loads.append(pltpu.make_async_copy(src, dst, load_sem.at[1 + i]))
-    stores = [pltpu.make_async_copy(src, dst, store_sem.at[i]) for i, (_, src, dst) in enumerate(stats + through)]
-    for load in loads:
-        load.start()
-    loads[0].wait()
-    for w, ref in enumerate((left, right)):
-        loads[1 + w].wait()
+    through = [(first, first_out), (second, second_out), (update, update_out)]
+    stats = [(new_left, left_out), (new_right, right_out)]
+    stores = [pltpu.make_async_copy(src, dst, sem.at[i]) for i, (src, dst) in enumerate(stats + through)]
+    for store in stores[2:]:
+        store.start()
+    for w, (old, new) in enumerate(((left, new_left), (right, new_right))):
 
         def add(slot, carry):
             code = prod[slot, pl.ds(2 * WIDE, T), :].astype(F32)[w * (T // 2) : (w + 1) * (T // 2)]
-            for t, value in enumerate(decode_rows(prod.at[slot], w * WIDE, jnp.exp(code * STEP) * (1.0 / FULL))):
-                ref[slot, :, pl.ds(t * LANES, LANES)] += value
+            scale = jnp.exp(code * STEP) * (1.0 / FULL)
+            for t, value in enumerate(decode_rows(prod.at[slot], w * WIDE, scale)):
+                cols = pl.ds(t * LANES, LANES)
+                new[slot, :, cols] = old[slot, :, cols] + value
             return carry
 
         lax.fori_loop(0, NB, add, 0)
         stores[w].start()
-    for i in range(len(through)):
-        loads[3 + i].wait()
-        stores[2 + i].start()
     for store in stores:
         store.wait()
 
@@ -420,6 +405,7 @@
     grad_parts, home, left_stat, right_stat, left_root, right_root, first_moment, second_moment
 ):
     in_hbm = pl.BlockSpec(memory_space=pltpu.HBM)
+    in_vmem = pl.BlockSpec(memory_space=pltpu.VMEM)
     n = len(PEERS)
     xpiece = (H // LANES * XROWS + T, LANES)
     ypiece = (H // LANES * YROWS + T, LANES)
@@ -431,8 +417,7 @@
     scratch = [
         pltpu.SMEM((NB,), I32),
         pltpu.VMEM((NB, B, H), F32),
-        *[stat] * 4,
-        tile,
+        *[stat] * 2,
         *[pltpu.VMEM((NB, 2, S, B), BF16)] * 2,
         *[pltpu.VMEM((4, *xpiece), I16)] * 2,
         *[pltpu.VMEM((6, *ypiece), I16)] * 2,
@@ -457,29 +442,33 @@
         *[dma((6,))] * 2,
         *[dma((3, n))] * 2,
         *[dma((n + 1,))] * 2,
-        dma((5,)),
+        dma((2,)),
     ]
-    stat_out = jax.ShapeDtypeStruct((NB, S, B), F32)
-    tile_out = jax.ShapeDtypeStruct((B, H), BF16)
     made = pl.pallas_call(
         kernel,
-        out_shape=(jax.ShapeDtypeStruct((NB, *products), I16), stat_out, stat_out, tile_out),
+        out_shape=(pltpu.VMEM((NB, *products), I16), stat, stat, tile),
         in_specs=[in_hbm] * 6,
-        out_specs=[in_hbm] * 4,
+        out_specs=[in_vmem] * 4,
         scratch_shapes=scratch,
         compiler_params=pltpu.CompilerParams(
-            collective_id=0, has_side_effects=True, vmem_limit_bytes=58 * 2**20
+            collective_id=0, has_side_effects=True, vmem_limit_bytes=40 * 2**20
         ),
         cost_estimate=pl.CostEstimate(flops=2 * 10**9, bytes_accessed=9 * 2**20, transcendentals=0),
         name="shampoo_step",
-    )(home, grad_parts.reshape(NB, B, H), left_root, right_root, first_moment, second_moment)
+    )(
+        *[
+            pltpu.with_memory_space_constraint(x, pltpu.HBM)
+            for x in (home, grad_parts.reshape(NB, B, H), left_root, right_root, first_moment, second_moment)
+        ]
+    )
+    stat_out = jax.ShapeDtypeStruct((NB, S, B), F32)
     return pl.pallas_call(
         finish_kernel,
-        out_shape=(stat_out,) * 4 + (tile_out,),
-        in_specs=[in_hbm] * 6,
+        out_shape=(stat_out,) * 4 + (jax.ShapeDtypeStruct((B, H), BF16),),
+        in_specs=[in_vmem] * 6,
         out_specs=[in_hbm] * 5,
-        scratch_shapes=[pltpu.VMEM((NB, *products), I16), *[stat] * 4, tile, dma((6,)), dma((5,))],
-        compiler_params=pltpu.CompilerParams(vmem_limit_bytes=58 * 2**20),
+        scratch_shapes=[stat, stat, dma((5,))],
+        compiler_params=pltpu.CompilerParams(vmem_limit_bytes=16 * 2**20),
         name="finish_outputs",
     )(made[0], left_stat, right_stat, *made[1:])
 

time: 49.4 us -> 48.1 us (0.974)
  Pallas kernels: 48.6 us -> 47.3 us
    pallas_call x2, Pallas kernels: 48.6 us -> 47.3 us  [the longest x1 45.9 us: on_device(): pl.pallas_call(kernel, out_shape=(pltpu.VMEM((NB, *products), I16), stat,...]
where the time goes in v5:
time: 48.1 us; the launch traced here: 48 us
  Pallas kernels  47.3 us (98%)
  between operations  0.67 us (1%)
    pallas_call x1, Pallas kernels, on_device(): pl.pallas_call(kernel, out_shape=(pltpu.VMEM((NB, *products), I16), stat,...  45.9 us
    pallas_call x1, Pallas kernels, on_device(): pl.pallas_call(finish_kernel, out_shape=(stat_out,) * 4 + (jax.ShapeDtype...  1.45 us

profile of v5, /device:TPU:1, one launch (start us, length us, event | category | flops | bytes accessed | tf_op | source)
XLA Modules:
  0.0 48.0 jit_solution(2622609086768020317)
XLA Ops:
  0.6 0.0 copy-start.1
  0.6 0.0 copy-start
  0.7 45.9 %shampoo_step.1 = (s16[8,272,128]{2,1,0:T(8,128)(2,1)S(1)}, f32[8,32,512]{2,1,0:T(8,128)S(1)}, f32[8,32,512]{2,1,0:T(8,128)S(1)}, bf16[512,256]{1,0:T(8,128)(2,1)S(1)}) custom-call(s32[8]{0:T(128)} %home_hbm.1, f32[8,512,256]{2,1,0:T(8,128)} %bitcast.1, bf16[8,32,512]{2,1,0:T(8,128)(2,1)} %lroot_hbm.1, bf16[8,32,512]{2,1,0:T(8,128)(2,1)} %rroot_hbm.1, ...), custom_call_target="tpu_custom_call" | custom-call | flops 2000000000 | bytes 9437184 | tf_op jit(solution)/shard_map/shampoo_step/pallas_call | solution.py:447
  46.5 0.0 copy-done.1
  46.5 0.0 copy-done
  46.5 1.4 %finish_outputs.1 = (f32[8,32,512]{2,1,0:T(8,128)}, f32[8,32,512]{2,1,0:T(8,128)}, f32[8,32,512]{2,1,0:T(8,128)}, f32[8,32,512]{2,1,0:T(8,128)}, bf16[512,256]{1,0:T(8,128)(2,1)}) custom-call(s16[8,272,128]{2,1,0:T(8,128)(2,1)S(1)} %get-tuple-element.9.prod, f32[8,32,512]{2,1,0:T(8,128)S(1)} %copy-done, f32[8,32,512]{2,1,0:T(8,128)S(1)} %copy-done.1, ...), custom_call_target="tpu_custom_call" | custom-call | tf_op jit(solution)/shard_map/finish_outputs/pallas_call | solution.py:465
Async XLA Ops:
  0.6 45.9 %copy-start.1 = (f32[8,32,512]{2,1,0:T(8,128)S(1)}, f32[8,32,512]{2,1,0:T(8,128)}, u32[]{:S(2)}) copy-start(f32[8,32,512]{2,1,0:T(8,128)} %right.1) | copy-start | bytes 1572868
  0.6 45.9 %copy-start = (f32[8,32,512]{2,1,0:T(8,128)S(1)}, f32[8,32,512]{2,1,0:T(8,128)}, u32[]{:S(2)}) copy-start(f32[8,32,512]{2,1,0:T(8,128)} %left.1) | copy-start | bytes 1572868

commit v6 on v5

--- a/solution.py
+++ b/solution.py
@@ -20,8 +20,9 @@
 
 B = 512
 H = 256
-XROWS = 192
-YROWS = B - XROWS
+PARTS = ((0, 192), (192, 192), (384, 128))
+RING = PARTS[0][1]
+CROSS = PARTS[2][1]
 S = 32
 T = 16
 STRIDE = 64
@@ -128,11 +129,11 @@
 def kernel(
     home_hbm, part_hbm, lroot_hbm, rroot_hbm, first_hbm, second_hbm,
     prod_in, new_first, new_second, update,
-    home, part, first, second, lroot, rroot,
-    x1_out, x1_in, y1_out, y1_in, x2_out, x2_in, y2_out, y2_in,
+    home, part_up, part_down, part_cross, first, second, lroot, rroot,
+    ring_out, ring_in, x1_out, x1_in, y2_out, y2_in, x2_out, x2_in,
     work, ghigh, glow, grow_out, grow_in, prod_out, left_codes, pleft, pright,
     sums_out, sums_in, pair_out, pair_in,
-    load_sem, root_send, root_recv, x1_send, x1_recv, y1_send, y1_recv, s2_send, s2_recv,
+    load_sem, root_send, root_recv, ring_send, ring_recv, x1_send, x1_recv, s2_send, s2_recv,
     core_send, core_recv, row_send, row_recv, sum_send, sum_recv, store_sem,
 ):
     d = lax.axis_index("dp")
@@ -158,17 +159,15 @@
             src_ref=src, dst_ref=dst, send_sem=send, recv_sem=recv, device_id=device, device_id_type=MESH
         )
 
-    loads = [
-        pltpu.make_async_copy(src, dst, load_sem.at[i])
-        for i, (src, dst) in enumerate(
-            [
-                (home_hbm, home), (part_hbm, part), (first_hbm, first), (second_hbm, second),
-                (lroot_hbm.at[c], lroot.at[c, k]), (rroot_hbm.at[c], rroot.at[c, k]),
-            ]
-        )
-    ]
-    loads[0].start()
-    loads[1].start()
+    parts = (part_up, part_down, part_cross)
+    loads = [pltpu.make_async_copy(home_hbm, home, load_sem.at[0])]
+    for i, (start, n) in enumerate(PARTS):
+        loads.append(pltpu.make_async_copy(part_hbm.at[:, pl.ds(start, n)], parts[i], load_sem.at[1 + i]))
+    others = ((lroot_hbm.at[c], lroot.at[c, k]), (rroot_hbm.at[c], rroot.at[c, k]), (first_hbm, first), (second_hbm, second))
+    for i, (src, dst) in enumerate(others):
+        loads.append(pltpu.make_async_copy(src, dst, load_sem.at[4 + i]))
+    for load in loads[:4]:
+        load.start()
 
     barrier = pltpu.get_barrier_semaphore()
     greeted = [partner, across] + [along_y(j) for j in (1, 2, 3)] + [along_mp(a, b) for a, b in PEERS]
@@ -177,58 +176,91 @@
     pl.semaphore_wait(barrier, len(greeted))
 
     root_copies = []
-    for i, (a, b) in enumerate(PEERS):
-        there = chip_at(a, b)
-        for w, (src, dst) in enumerate(((lroot_hbm, lroot), (rroot_hbm, rroot))):
-            copy = remote(src.at[there], dst.at[c, k], root_send.at[w, i], root_recv.at[w, i], along_mp(a, b))
-            copy.start()
-            root_copies.append(copy)
-    for load in loads[2:]:
-        load.start()
+
+    def send_roots(wanted):
+        for i, (a, b) in enumerate(PEERS):
+            if a == wanted:
+                there = chip_at(a, b)
+                for w, (src, dst) in enumerate(((lroot_hbm, lroot), (rroot_hbm, rroot))):
+                    copy = remote(
+                        src.at[there], dst.at[c, k], root_send.at[w, i], root_recv.at[w, i], along_mp(a, b)
+                    )
+                    copy.start()
+                    root_copies.append(copy)
 
     def source(q):
         return functools.reduce(jnp.maximum, [jnp.where(home[r] == q, r, 0) for r in range(NB)])
 
-    def own_piece(to_x, j, start):
+    def own_piece(w, to_x, j):
         row = source(to_x * NY + (y + j) % NY)
-        return lambda t, r: part[row, pl.ds(start + r, STRIDE), pl.ds(t * LANES, LANES)]
-
+        return lambda t, r: parts[w][row, pl.ds(r, STRIDE), pl.ds(t * LANES, LANES)]
+
+    to_xs = (1 - xl, xl)
+    along = (1, -1)
+    ring = {}
+
+    def send_ring(kind, w, o, to, step, arrived):
+        n = (kind * 2 + w) * 2 + o
+        own = own_piece(w, to_xs[o], to)
+        if arrived:
+            encode_piece(RING, sum_of(RING, own, arrived), ring_out.at[n], work)
+        else:
+            encode_piece(RING, own, ring_out.at[n])
+        ring[kind, w, o] = remote(
+            ring_out.at[n], ring_in.at[n], ring_send.at[n], ring_recv.at[n], along_y(step % NY)
+        )
+        ring[kind, w, o].start()
+
+    def got(kind, w, o):
+        ring[kind, w, o].wait_recv()
+        return ring_in.at[(kind * 2 + w) * 2 + o]
+
+    def send_far(w, o):
+        send_ring(0, w, o, 2, along[w], [])
+
+    def send_back(w, o):
+        send_ring(1, w, o, -along[w], -along[w], [])
+
+    def send_on(w, o):
+        send_ring(2, w, o, along[w], along[w], [got(0, w, o)])
+
+    send_roots(0)
     loads[0].wait()
     loads[1].wait()
-    x1_copies, y1_copies = {}, {}
-
-    def send_x1(j):
-        encode_piece(XROWS, own_piece(1 - xl, j, YROWS), x1_out.at[j])
+    send_far(0, 0)
+    loads[2].wait()
+    send_far(1, 0)
+    loads[3].wait()
+    x1_copies, y2_copies, x2_copies = {}, {}, {}
+    for j in (2, 1, 3, 0):
+        encode_piece(CROSS, own_piece(2, 1 - xl, j), x1_out.at[j])
         x1_copies[j] = remote(x1_out.at[j], x1_in.at[j], x1_send.at[j], x1_recv.at[j], across)
         x1_copies[j].start()
-
-    def send_y1(w, j):
-        n = w * 3 + j - 1
-        encode_piece(YROWS, own_piece(1 - xl if w == 0 else xl, j, 0), y1_out.at[n])
-        y1_copies[w, j] = remote(y1_out.at[n], y1_in.at[n], y1_send.at[n], y1_recv.at[n], along_y(j))
-        y1_copies[w, j].start()
-
-    for j in (1, 3, 2):
-        send_y1(0, j)
-        send_x1(j)
-    for j in (1, 3, 2):
-        send_y1(1, j)
-    send_x1(0)
-
-    y2_copies = {}
-    for j in (1, 3, 2):
+        if j == 2:
+            for w in range(2):
+                send_far(w, 1)
+    for load in loads[4:]:
+        load.start()
+    send_roots(1)
+    send_back(1, 0)
+    send_back(0, 0)
+    send_on(0, 0)
+    send_on(1, 0)
+    send_back(1, 1)
+    send_back(0, 1)
+    send_on(0, 1)
+    send_on(1, 1)
+    for j in (2, 1, 3):
         x1_copies[j].wait_recv()
-        read = sum_of(XROWS, own_piece(xl, j, YROWS), [x1_in.at[j]])
-        encode_piece(XROWS, read, y2_out.at[j - 1], work)
+        read = sum_of(CROSS, own_piece(2, xl, j), [x1_in.at[j]])
+        encode_piece(CROSS, read, y2_out.at[j - 1], work)
         y2_copies[j] = remote(y2_out.at[j - 1], y2_in.at[j - 1], s2_send.at[j], s2_recv.at[j], along_y(j))
         y2_copies[j].start()
-
-    for j in (1, 2, 3):
-        y1_copies[0, j].wait_recv()
-    read = sum_of(YROWS, own_piece(1 - xl, 0, 0), [y1_in.at[n] for n in range(3)])
-    encode_piece(YROWS, read, x2_out, work)
-    x2_copy = remote(x2_out, x2_in, s2_send.at[0], s2_recv.at[0], across)
-    x2_copy.start()
+    for w in range(2):
+        read = sum_of(RING, own_piece(w, 1 - xl, 0), [got(1, w, 0), got(2, w, 0)])
+        encode_piece(RING, read, x2_out.at[w], work)
+        x2_copies[w] = remote(x2_out.at[w], x2_in.at[w], s2_send.at[4 * w], s2_recv.at[4 * w], across)
+        x2_copies[w].start()
 
     for copy in root_copies:
         copy.wait_recv()
@@ -241,9 +273,12 @@
         core_copies.append(copy)
 
     strip = pl.ds(pl.multiple_of(k * H, H), H)
-    block_copies = []
-
-    def finish(n, start, read, w):
+    block_copies = {}
+
+    def finish(w, arrived):
+        start, n = PARTS[w]
+        read = sum_of(n, own_piece(w, xl, 0), arrived)
+
         def step(i, carry):
             r = pl.multiple_of(i * STRIDE, STRIDE)
             for t in range(H // LANES):
@@ -256,37 +291,44 @@
         lax.fori_loop(0, n // STRIDE, step, 0)
         for i, ref in enumerate((ghigh, glow)):
             here = ref.at[pl.ds(start, n), strip]
-            copy = remote(here, here, core_send.at[2 + 2 * w + i], core_recv.at[2 + 2 * w + i], partner)
-            copy.start()
-            block_copies.append(copy)
-
-    x1_copies[0].wait_recv()
-    for j in (1, 3, 2):
-        y2_copies[j].wait_recv()
-    arrived = [x1_in.at[0]] + [y2_in.at[n] for n in range(3)]
-    finish(XROWS, YROWS, sum_of(XROWS, own_piece(xl, 0, YROWS), arrived), 0)
-    for j in (1, 2, 3):
-        y1_copies[1, j].wait_recv()
-    x2_copy.wait_recv()
-    arrived = [y1_in.at[n] for n in range(3, 6)] + [x2_in]
-    finish(YROWS, 0, sum_of(YROWS, own_piece(xl, 0, 0), arrived), 1)
-
-    for copy in block_copies:
-        copy.wait_recv()
+            n_sem = 2 + 2 * w + i
+            block_copies[w, i] = remote(here, here, core_send.at[n_sem], core_recv.at[n_sem], partner)
+            block_copies[w, i].start()
 
     def rows_for(there):
         return pl.ds(pl.multiple_of(there * 2 * S + k * S, S), S)
 
-    row_copies = []
-    for i, (a, b) in enumerate(PEERS + [(0, 0)]):
-        rows = rows_for(chip_at(a, b))
-        value = ghigh[rows, :].astype(F32) + glow[rows, :].astype(F32)
-        out = grow_out.at[i] if a or b else grow_in.at[c]
-        out[pl.ds(WIDE, T), :] = encode_rows(value, T, out, 0).astype(I32).astype(I16)
-        if a or b:
-            copy = remote(out, grow_in.at[c], row_send.at[0, i], row_recv.at[0, i], along_mp(a, b))
-            copy.start()
-            row_copies.append(copy)
+    def row_copy(there, slot):
+        return remote(
+            grow_out.at[there], grow_in.at[slot], row_send.at[0, there], row_recv.at[0, slot], (d, there * 2 + k)
+        )
+
+    def send_rows(w):
+        for i in range(2):
+            block_copies[w, i].wait_recv()
+        start, n = PARTS[w]
+        for there in range(start // (2 * S), (start + n) // (2 * S)):
+            rows = rows_for(there)
+            value = ghigh[rows, :].astype(F32) + glow[rows, :].astype(F32)
+            code = encode_rows(value, T, grow_out.at[there], 0)
+            grow_out[there, pl.ds(WIDE, T), :] = code.astype(I32).astype(I16)
+
+            @pl.when(c != there)
+            def _():
+                row_copy(there, c).start()
+
+    for w in range(2):
+        x2_copies[w].wait_recv()
+        finish(w, [got(1, w, 1), got(2, w, 1), x2_in.at[w]])
+        if w:
+            send_rows(0)
+    x1_copies[0].wait_recv()
+    for j in (2, 1, 3):
+        y2_copies[j].wait_recv()
+    finish(2, [x1_in.at[0]] + [y2_in.at[n] for n in range(3)])
+    send_rows(1)
+    send_rows(2)
+    grow_in[c] = grow_out[c]
 
     high_rows = jnp.concatenate([ghigh[rows_for(t), :] for t in range(NB)], axis=0)
     low_rows = jnp.concatenate([glow[rows_for(t), :] for t in range(NB)], axis=0)
@@ -319,13 +361,13 @@
         codes = jnp.concatenate([left_codes[i], code], axis=0)
         prod_out[i, pl.ds(2 * WIDE, T), :] = codes.astype(I32).astype(I16)
 
-    loads[2].wait()
-    loads[3].wait()
+    loads[6].wait()
+    loads[7].wait()
     sum_copies = []
     for i, (a, b) in enumerate(PEERS + [(0, 0)]):
         slot = chip_at(-a, -b)
         if a or b:
-            row_copies[i].wait_recv()
+            row_copy(slot, slot).wait_recv()
         total = jnp.zeros((8, LANES), F32)
         scale = scale_of(grow_in[slot, pl.ds(WIDE, T), :])
         for t, grad in enumerate(decode_rows(grow_in.at[slot], 0, scale)):
@@ -368,8 +410,12 @@
 
     for copy in prod_copies:
         copy.wait_recv()
-    sent = [x2_copy, pair_copy] + root_copies + core_copies + block_copies + row_copies + prod_copies + sum_copies
-    for copy in sent + list(x1_copies.values()) + list(y1_copies.values()) + list(y2_copies.values()):
+    for a, b in PEERS:
+        row_copy(chip_at(a, b), c).wait_send()
+    for copies in (x1_copies, y2_copies, x2_copies, ring, block_copies):
+        for copy in copies.values():
+            copy.wait_send()
+    for copy in [pair_copy] + root_copies + core_copies + prod_copies + sum_copies:
         copy.wait_send()
     for store in stores:
         store.wait()
@@ -407,8 +453,8 @@
     in_hbm = pl.BlockSpec(memory_space=pltpu.HBM)
     in_vmem = pl.BlockSpec(memory_space=pltpu.VMEM)
     n = len(PEERS)
-    xpiece = (H // LANES * XROWS + T, LANES)
-    ypiece = (H // LANES * YROWS + T, LANES)
+    ring_piece = (H // LANES * RING + T, LANES)
+    cross_piece = (H // LANES * CROSS + T, LANES)
     rows = (WIDE + T, LANES)
     products = (2 * WIDE + T, LANES)
     stat = pltpu.VMEM((NB, S, B), F32)
@@ -416,17 +462,16 @@
     dma = pltpu.SemaphoreType.DMA
     scratch = [
         pltpu.SMEM((NB,), I32),
-        pltpu.VMEM((NB, B, H), F32),
+        *[pltpu.VMEM((NB, size, H), F32) for _, size in PARTS],
         *[stat] * 2,
         *[pltpu.VMEM((NB, 2, S, B), BF16)] * 2,
-        *[pltpu.VMEM((4, *xpiece), I16)] * 2,
-        *[pltpu.VMEM((6, *ypiece), I16)] * 2,
-        *[pltpu.VMEM(ypiece, I16)] * 2,
-        *[pltpu.VMEM((3, *xpiece), I16)] * 2,
+        *[pltpu.VMEM((12, *ring_piece), I16)] * 2,
+        *[pltpu.VMEM((4, *cross_piece), I16)] * 2,
+        *[pltpu.VMEM((3, *cross_piece), I16)] * 2,
+        *[pltpu.VMEM((2, *ring_piece), I16)] * 2,
         pltpu.VMEM((B, H), F32),
         *[pltpu.VMEM((B, B), BF16)] * 2,
-        pltpu.VMEM((n, *rows), I16),
-        pltpu.VMEM((NB, *rows), I16),
+        *[pltpu.VMEM((NB, *rows), I16)] * 2,
         pltpu.VMEM((NB, *products), I16),
         pltpu.VMEM((NB, T // 2, LANES), F32),
         pltpu.VMEM((H, B), F32),
@@ -434,13 +479,13 @@
         pltpu.VMEM((NB, 8, LANES), F32),
         pltpu.VMEM((n, 8, LANES), F32),
         *[pltpu.VMEM((2, 8, LANES), F32)] * 2,
-        dma((6,)),
+        dma((8,)),
         *[dma((2, n))] * 2,
+        *[dma((12,))] * 2,
         *[dma((4,))] * 2,
-        *[dma((6,))] * 2,
-        *[dma((4,))] * 2,
-        *[dma((6,))] * 2,
-        *[dma((3, n))] * 2,
+        *[dma((5,))] * 2,
+        *[dma((8,))] * 2,
+        *[dma((3, NB))] * 2,
         *[dma((n + 1,))] * 2,
         dma((2,)),
     ]

time: 48.1 us -> 45.6 us (0.948)
  Pallas kernels: 47.3 us -> 44.8 us
    pallas_call x1, Pallas kernels: 45.9 us -> 43.4 us  [on_device(): pl.pallas_call(kernel, out_shape=(pltpu.VMEM((NB, *products), I16), stat,...]
where the time goes in v6:
time: 45.6 us; the launch traced here: 45.5 us
  Pallas kernels  44.8 us (98%)
  between operations  0.67 us (1%)
    pallas_call x1, Pallas kernels, on_device(): pl.pallas_call(kernel, out_shape=(pltpu.VMEM((NB, *products), I16), stat,...  43.4 us
    pallas_call x1, Pallas kernels, on_device(): pl.pallas_call(finish_kernel, out_shape=(stat_out,) * 4 + (jax.ShapeDtype...  1.45 us

profile of v6, /device:TPU:1, one launch (start us, length us, event | category | flops | bytes accessed | tf_op | source)
XLA Modules:
  0.0 45.5 jit_solution(9925433888088056227)
XLA Ops:
  0.6 0.0 copy-start.1
  0.6 0.0 copy-start
  0.7 43.4 %shampoo_step.1 = (s16[8,272,128]{2,1,0:T(8,128)(2,1)S(1)}, f32[8,32,512]{2,1,0:T(8,128)S(1)}, f32[8,32,512]{2,1,0:T(8,128)S(1)}, bf16[512,256]{1,0:T(8,128)(2,1)S(1)}) custom-call(s32[8]{0:T(128)} %home_hbm.1, f32[8,512,256]{2,1,0:T(8,128)} %bitcast.1, bf16[8,32,512]{2,1,0:T(8,128)(2,1)} %lroot_hbm.1, bf16[8,32,512]{2,1,0:T(8,128)(2,1)} %rroot_hbm.1, ...), custom_call_target="tpu_custom_call" | custom-call | flops 2000000000 | bytes 9437184 | tf_op jit(solution)/shard_map/shampoo_step/pallas_call | solution.py:492
  44.1 0.0 copy-done.1
  44.1 0.0 copy-done
  44.1 1.4 %finish_outputs.1 = (f32[8,32,512]{2,1,0:T(8,128)}, f32[8,32,512]{2,1,0:T(8,128)}, f32[8,32,512]{2,1,0:T(8,128)}, f32[8,32,512]{2,1,0:T(8,128)}, bf16[512,256]{1,0:T(8,128)(2,1)}) custom-call(s16[8,272,128]{2,1,0:T(8,128)(2,1)S(1)} %get-tuple-element.9.prod, f32[8,32,512]{2,1,0:T(8,128)S(1)} %copy-done, f32[8,32,512]{2,1,0:T(8,128)S(1)} %copy-done.1, ...), custom_call_target="tpu_custom_call" | custom-call | tf_op jit(solution)/shard_map/finish_outputs/pallas_call | solution.py:510
Async XLA Ops:
  0.6 43.4 %copy-start.1 = (f32[8,32,512]{2,1,0:T(8,128)S(1)}, f32[8,32,512]{2,1,0:T(8,128)}, u32[]{:S(2)}) copy-start(f32[8,32,512]{2,1,0:T(8,128)} %right.1) | copy-start | bytes 1572868
  0.6 43.4 %copy-start = (f32[8,32,512]{2,1,0:T(8,128)S(1)}, f32[8,32,512]{2,1,0:T(8,128)}, u32[]{:S(2)}) copy-start(f32[8,32,512]{2,1,0:T(8,128)} %left.1) | copy-start | bytes 1572868

commit v7 on v6

--- a/solution.py
+++ b/solution.py
@@ -132,7 +132,7 @@
     home, part_up, part_down, part_cross, first, second, lroot, rroot,
     ring_out, ring_in, x1_out, x1_in, y2_out, y2_in, x2_out, x2_in,
     work, ghigh, glow, grow_out, grow_in, prod_out, left_codes, pleft, pright,
-    sums_out, sums_in, pair_out, pair_in,
+    sums_out, sums_other, sums_chip, sums_in, pair_out, pair_in,
     load_sem, root_send, root_recv, ring_send, ring_recv, x1_send, x1_recv, s2_send, s2_recv,
     core_send, core_recv, row_send, row_recv, sum_send, sum_recv, store_sem,
 ):
@@ -361,10 +361,25 @@
         codes = jnp.concatenate([left_codes[i], code], axis=0)
         prod_out[i, pl.ds(2 * WIDE, T), :] = codes.astype(I32).astype(I16)
 
+    for i in range(NB):
+        send_products(1, i, WIDE, WIDE + T)
+
+    for copy in core_copies:
+        copy.wait_recv()
+    rcols = jnp.concatenate([rroot[a, b, :, strip] for a in range(NB) for b in range(2)], axis=0)
+    inner = dot(ghigh[...], rcols) + dot(glow[...], rcols)
+    inner_high, inner_low = split(inner)
+    lrows = lroot[...].reshape(B, B)
+    applied = dot(lrows, inner_high) + dot(lrows, inner_low)
+    pright[:, pl.ds(0, H)] = applied
+    pair_out[...] = fold(applied * applied)
+    n = len(PEERS)
+    pair_copy = remote(pair_out, pair_in, sum_send.at[n], sum_recv.at[n], partner)
+    pair_copy.start()
+
     loads[6].wait()
     loads[7].wait()
-    sum_copies = []
-    for i, (a, b) in enumerate(PEERS + [(0, 0)]):
+    for a, b in PEERS + [(0, 0)]:
         slot = chip_at(-a, -b)
         if a or b:
             row_copy(slot, slot).wait_recv()
@@ -378,33 +393,24 @@
             new_second[slot, :, cols] = square
             adam = mean / (jnp.sqrt(square) + ADAM_EPS)
             total = total + fold(adam * adam)
-        sums_out[i] = total
-        if a or b:
-            copy = remote(sums_out.at[i], sums_in.at[i], sum_send.at[i], sum_recv.at[i], along_mp(-a, -b))
-            copy.start()
-            sum_copies.append(copy)
-    for i in range(NB):
-        send_products(1, i, WIDE, WIDE + T)
-
-    for copy in core_copies:
-        copy.wait_recv()
-    rcols = jnp.concatenate([rroot[a, b, :, strip] for a in range(NB) for b in range(2)], axis=0)
-    inner = dot(ghigh[...], rcols) + dot(glow[...], rcols)
-    inner_high, inner_low = split(inner)
-    lrows = lroot[...].reshape(B, B)
-    applied = dot(lrows, inner_high) + dot(lrows, inner_low)
-    pright[:, pl.ds(0, H)] = applied
-    pair_out[1] = fold(applied * applied)
-
-    total = sums_out[len(PEERS)]
+        sums_out[slot] = total
+
+    chip_copy = remote(sums_out, sums_other, sum_send.at[n + 1], sum_recv.at[n + 1], partner)
+    chip_copy.start()
+    chip_copy.wait_recv()
+    sums_chip[...] = sums_out[...] + sums_other[...]
+    sum_copies = []
+    for i, (a, b) in enumerate(PEERS):
+        copy = remote(sums_chip.at[chip_at(a, b)], sums_in.at[i], sum_send.at[i], sum_recv.at[i], along_mp(a, b))
+        copy.start()
+        sum_copies.append(copy)
+
+    pair_copy.wait_recv()
+    total = sums_chip[c]
     for i, copy in enumerate(sum_copies):
         copy.wait_recv()
         total = total + sums_in[i]
-    pair_out[0] = total
-    pair_copy = remote(pair_out, pair_in, sum_send.at[len(PEERS)], sum_recv.at[len(PEERS)], partner)
-    pair_copy.start()
-    pair_copy.wait_recv()
-    norms = [jnp.sum(pair_out[w] + pair_in[w], axis=(0, 1), keepdims=True) for w in range(2)]
+    norms = [jnp.sum(x, axis=(0, 1), keepdims=True) for x in (total, pair_out[...] + pair_in[...])]
     graft = jnp.sqrt(norms[0]) / (jnp.sqrt(norms[1]) + NORM_EPS)
     update[...] = (pright[:, pl.ds(0, H)] * graft).astype(BF16)
 
@@ -415,7 +421,7 @@
     for copies in (x1_copies, y2_copies, x2_copies, ring, block_copies):
         for copy in copies.values():
             copy.wait_send()
-    for copy in [pair_copy] + root_copies + core_copies + prod_copies + sum_copies:
+    for copy in [pair_copy, chip_copy] + root_copies + core_copies + prod_copies + sum_copies:
         copy.wait_send()
     for store in stores:
         store.wait()
@@ -476,9 +482,9 @@
         pltpu.VMEM((NB, T // 2, LANES), F32),
         pltpu.VMEM((H, B), F32),
         pltpu.VMEM((B, B), F32),
-        pltpu.VMEM((NB, 8, LANES), F32),
+        *[pltpu.VMEM((NB, 8, LANES), F32)] * 3,
         pltpu.VMEM((n, 8, LANES), F32),
-        *[pltpu.VMEM((2, 8, LANES), F32)] * 2,
+        *[pltpu.VMEM((8, LANES), F32)] * 2,
         dma((8,)),
         *[dma((2, n))] * 2,
         *[dma((12,))] * 2,
@@ -486,7 +492,7 @@
         *[dma((5,))] * 2,
         *[dma((8,))] * 2,
         *[dma((3, NB))] * 2,
-        *[dma((n + 1,))] * 2,
+        *[dma((n + 2,))] * 2,
         dma((2,)),
     ]
     made = pl.pallas_call(

time: 45.6 us -> 45.4 us (level)
  no operation moved by 1% of the time
where the time goes in v7:
time: 45.4 us; the launch traced here: 45.3 us
  Pallas kernels  44.6 us (98%)
  between operations  0.67 us (1%)
    pallas_call x1, Pallas kernels, on_device(): pl.pallas_call(kernel, out_shape=(pltpu.VMEM((NB, *products), I16), stat,...  43.2 us
    pallas_call x1, Pallas kernels, on_device(): pl.pallas_call(finish_kernel, out_shape=(stat_out,) * 4 + (jax.ShapeDtype...  1.45 us

profile of v7, /device:TPU:1, one launch (start us, length us, event | category | flops | bytes accessed | tf_op | source)
XLA Modules:
  0.0 45.3 jit_solution(14599301292909215738)
XLA Ops:
  0.6 0.0 copy-start.1
  0.6 0.0 copy-start
  0.7 43.2 %shampoo_step.1 = (s16[8,272,128]{2,1,0:T(8,128)(2,1)S(1)}, f32[8,32,512]{2,1,0:T(8,128)S(1)}, f32[8,32,512]{2,1,0:T(8,128)S(1)}, bf16[512,256]{1,0:T(8,128)(2,1)S(1)}) custom-call(s32[8]{0:T(128)} %home_hbm.1, f32[8,512,256]{2,1,0:T(8,128)} %bitcast.1, bf16[8,32,512]{2,1,0:T(8,128)(2,1)} %lroot_hbm.1, bf16[8,32,512]{2,1,0:T(8,128)(2,1)} %rroot_hbm.1, ...), custom_call_target="tpu_custom_call" | custom-call | flops 2000000000 | bytes 9437184 | tf_op jit(solution)/shard_map/shampoo_step/pallas_call | solution.py:498
  43.8 0.0 copy-done.1
  43.8 0.0 copy-done
  43.9 1.4 %finish_outputs.1 = (f32[8,32,512]{2,1,0:T(8,128)}, f32[8,32,512]{2,1,0:T(8,128)}, f32[8,32,512]{2,1,0:T(8,128)}, f32[8,32,512]{2,1,0:T(8,128)}, bf16[512,256]{1,0:T(8,128)(2,1)}) custom-call(s16[8,272,128]{2,1,0:T(8,128)(2,1)S(1)} %get-tuple-element.9.prod, f32[8,32,512]{2,1,0:T(8,128)S(1)} %copy-done, f32[8,32,512]{2,1,0:T(8,128)S(1)} %copy-done.1, ...), custom_call_target="tpu_custom_call" | custom-call | tf_op jit(solution)/shard_map/finish_outputs/pallas_call | solution.py:516
Async XLA Ops:
  0.6 43.2 %copy-start.1 = (f32[8,32,512]{2,1,0:T(8,128)S(1)}, f32[8,32,512]{2,1,0:T(8,128)}, u32[]{:S(2)}) copy-start(f32[8,32,512]{2,1,0:T(8,128)} %right.1) | copy-start | bytes 1572868
  0.6 43.2 %copy-start = (f32[8,32,512]{2,1,0:T(8,128)S(1)}, f32[8,32,512]{2,1,0:T(8,128)}, u32[]{:S(2)}) copy-start(f32[8,32,512]{2,1,0:T(8,128)} %left.1) | copy-start | bytes 1572868

commit v8 on v7

--- a/solution.py
+++ b/solution.py
@@ -134,7 +134,7 @@
     work, ghigh, glow, grow_out, grow_in, prod_out, left_codes, pleft, pright,
     sums_out, sums_other, sums_chip, sums_in, pair_out, pair_in,
     load_sem, root_send, root_recv, ring_send, ring_recv, x1_send, x1_recv, s2_send, s2_recv,
-    core_send, core_recv, row_send, row_recv, sum_send, sum_recv, store_sem,
+    core_send, core_recv, row_send, row_recv, sum_send, sum_recv, store_sem, ready,
 ):
     d = lax.axis_index("dp")
     m = lax.axis_index("mp")
@@ -169,24 +169,43 @@
     for load in loads[:4]:
         load.start()
 
+    rank = 2 * z + xh
+
+    def rank_of(there):
+        return 2 * (there % 4) + there // 4
+
     barrier = pltpu.get_barrier_semaphore()
-    greeted = [partner, across] + [along_y(j) for j in (1, 2, 3)] + [along_mp(a, b) for a, b in PEERS]
-    for device in greeted:
+    for device in [across, partner] + [along_y(j) for j in (1, 2, 3)]:
         pl.semaphore_signal(barrier, inc=1, device_id=device, device_id_type=MESH)
-    pl.semaphore_wait(barrier, len(greeted))
+    for a, b in PEERS:
+
+        @pl.when(rank_of(chip_at(a, b)) > rank)
+        def _():
+            pl.semaphore_signal(barrier, inc=1, device_id=along_mp(a, b), device_id_type=MESH)
+
+    pl.semaphore_wait(barrier, 5 + rank)
+    for a, b in PEERS:
+
+        @pl.when(rank_of(chip_at(a, b)) < rank)
+        def _():
+            pl.semaphore_signal(ready, inc=1, device_id=along_mp(a, b), device_id_type=MESH)
 
     root_copies = []
-
-    def send_roots(wanted):
+    for i, (a, b) in enumerate(PEERS):
+        there = chip_at(a, b)
+        for w, (src, dst) in enumerate(((lroot_hbm, lroot), (rroot_hbm, rroot))):
+            root_copies.append(
+                remote(src.at[there], dst.at[c, k], root_send.at[w, i], root_recv.at[w, i], along_mp(a, b))
+            )
+
+    def send_roots(higher):
         for i, (a, b) in enumerate(PEERS):
-            if a == wanted:
-                there = chip_at(a, b)
-                for w, (src, dst) in enumerate(((lroot_hbm, lroot), (rroot_hbm, rroot))):
-                    copy = remote(
-                        src.at[there], dst.at[c, k], root_send.at[w, i], root_recv.at[w, i], along_mp(a, b)
-                    )
+            there = rank_of(chip_at(a, b))
+
+            @pl.when(there > rank if higher else there < rank)
+            def _():
+                for copy in root_copies[2 * i : 2 * i + 2]:
                     copy.start()
-                    root_copies.append(copy)
 
     def source(q):
         return functools.reduce(jnp.maximum, [jnp.where(home[r] == q, r, 0) for r in range(NB)])
@@ -224,7 +243,6 @@
     def send_on(w, o):
         send_ring(2, w, o, along[w], along[w], [got(0, w, o)])
 
-    send_roots(0)
     loads[0].wait()
     loads[1].wait()
     send_far(0, 0)
@@ -241,7 +259,7 @@
                 send_far(w, 1)
     for load in loads[4:]:
         load.start()
-    send_roots(1)
+    send_roots(False)
     send_back(1, 0)
     send_back(0, 0)
     send_on(0, 0)
@@ -256,6 +274,12 @@
         encode_piece(CROSS, read, y2_out.at[j - 1], work)
         y2_copies[j] = remote(y2_out.at[j - 1], y2_in.at[j - 1], s2_send.at[j], s2_recv.at[j], along_y(j))
         y2_copies[j].start()
+
+    @pl.when(rank < NB - 1)
+    def _():
+        pl.semaphore_wait(ready, NB - 1 - rank)
+
+    send_roots(True)
     for w in range(2):
         read = sum_of(RING, own_piece(w, 1 - xl, 0), [got(1, w, 0), got(2, w, 0)])
         encode_piece(RING, read, x2_out.at[w], work)
@@ -494,6 +518,7 @@
         *[dma((3, NB))] * 2,
         *[dma((n + 2,))] * 2,
         dma((2,)),
+        pltpu.SemaphoreType.REGULAR,
     ]
     made = pl.pallas_call(
         kernel,

time: 45.4 us -> 44 us (0.969)
  Pallas kernels: 44.6 us -> 43.2 us
    pallas_call x1, Pallas kernels: 43.2 us -> 41.7 us  [on_device(): pl.pallas_call(kernel, out_shape=(pltpu.VMEM((NB, *products), I16), stat,...]
where the time goes in v8:
time: 44 us; the launch traced here: 43.9 us
  Pallas kernels  43.2 us (98%)
  between operations  0.67 us (2%)
    pallas_call x1, Pallas kernels, on_device(): pl.pallas_call(kernel, out_shape=(pltpu.VMEM((NB, *products), I16), stat,...  41.7 us
    pallas_call x1, Pallas kernels, on_device(): pl.pallas_call(finish_kernel, out_shape=(stat_out,) * 4 + (jax.ShapeDtype...  1.45 us

profile of v8, /device:TPU:1, one launch (start us, length us, event | category | flops | bytes accessed | tf_op | source)
XLA Modules:
  0.0 43.9 jit_solution(14170265324531914861)
XLA Ops:
  0.6 0.0 copy-start.1
  0.6 0.0 copy-start
  0.7 41.7 %shampoo_step.1 = (s16[8,272,128]{2,1,0:T(8,128)(2,1)S(1)}, f32[8,32,512]{2,1,0:T(8,128)S(1)}, f32[8,32,512]{2,1,0:T(8,128)S(1)}, bf16[512,256]{1,0:T(8,128)(2,1)S(1)}) custom-call(s32[8]{0:T(128)} %home_hbm.1, f32[8,512,256]{2,1,0:T(8,128)} %bitcast.1, bf16[8,32,512]{2,1,0:T(8,128)(2,1)} %lroot_hbm.1, bf16[8,32,512]{2,1,0:T(8,128)(2,1)} %rroot_hbm.1, ...), custom_call_target="tpu_custom_call" | custom-call | flops 2000000000 | bytes 9437184 | tf_op jit(solution)/shard_map/shampoo_step/pallas_call | solution.py:523
  42.4 0.0 copy-done.1
  42.4 0.0 copy-done
  42.4 1.4 %finish_outputs.1 = (f32[8,32,512]{2,1,0:T(8,128)}, f32[8,32,512]{2,1,0:T(8,128)}, f32[8,32,512]{2,1,0:T(8,128)}, f32[8,32,512]{2,1,0:T(8,128)}, bf16[512,256]{1,0:T(8,128)(2,1)}) custom-call(s16[8,272,128]{2,1,0:T(8,128)(2,1)S(1)} %get-tuple-element.9.prod, f32[8,32,512]{2,1,0:T(8,128)S(1)} %copy-done, f32[8,32,512]{2,1,0:T(8,128)S(1)} %copy-done.1, ...), custom_call_target="tpu_custom_call" | custom-call | tf_op jit(solution)/shard_map/finish_outputs/pallas_call | solution.py:541
Async XLA Ops:
  0.6 41.8 %copy-start.1 = (f32[8,32,512]{2,1,0:T(8,128)S(1)}, f32[8,32,512]{2,1,0:T(8,128)}, u32[]{:S(2)}) copy-start(f32[8,32,512]{2,1,0:T(8,128)} %right.1) | copy-start | bytes 1572868
  0.6 41.8 %copy-start = (f32[8,32,512]{2,1,0:T(8,128)S(1)}, f32[8,32,512]{2,1,0:T(8,128)}, u32[]{:S(2)}) copy-start(f32[8,32,512]{2,1,0:T(8,128)} %left.1) | copy-start | bytes 1572868

commit v9 on v8

--- a/solution.py
+++ b/solution.py
@@ -198,14 +198,21 @@
                 remote(src.at[there], dst.at[c, k], root_send.at[w, i], root_recv.at[w, i], along_mp(a, b))
             )
 
-    def send_roots(higher):
+    def send_roots(early):
         for i, (a, b) in enumerate(PEERS):
-            there = rank_of(chip_at(a, b))
-
-            @pl.when(there > rank if higher else there < rank)
-            def _():
-                for copy in root_copies[2 * i : 2 * i + 2]:
-                    copy.start()
+            lower = rank_of(chip_at(a, b)) < rank
+            for w in range(2):
+
+                @pl.when(lower if early else jnp.logical_not(lower))
+                def _():
+                    if not (early and a and w):
+                        root_copies[2 * i + w].start()
+
+                if not early and a and w:
+
+                    @pl.when(lower)
+                    def _():
+                        root_copies[2 * i + w].start()
 
     def source(q):
         return functools.reduce(jnp.maximum, [jnp.where(home[r] == q, r, 0) for r in range(NB)])
@@ -259,7 +266,7 @@
                 send_far(w, 1)
     for load in loads[4:]:
         load.start()
-    send_roots(False)
+    send_roots(True)
     send_back(1, 0)
     send_back(0, 0)
     send_on(0, 0)
@@ -274,27 +281,17 @@
         encode_piece(CROSS, read, y2_out.at[j - 1], work)
         y2_copies[j] = remote(y2_out.at[j - 1], y2_in.at[j - 1], s2_send.at[j], s2_recv.at[j], along_y(j))
         y2_copies[j].start()
-
-    @pl.when(rank < NB - 1)
-    def _():
-        pl.semaphore_wait(ready, NB - 1 - rank)
-
-    send_roots(True)
     for w in range(2):
         read = sum_of(RING, own_piece(w, 1 - xl, 0), [got(1, w, 0), got(2, w, 0)])
         encode_piece(RING, read, x2_out.at[w], work)
         x2_copies[w] = remote(x2_out.at[w], x2_in.at[w], s2_send.at[4 * w], s2_recv.at[4 * w], across)
         x2_copies[w].start()
 
-    for copy in root_copies:
-        copy.wait_recv()
-    loads[4].wait()
-    loads[5].wait()
-    core_copies = []
-    for w, ref in enumerate((lroot, rroot)):
-        copy = remote(ref.at[:, k], ref.at[:, k], core_send.at[w], core_recv.at[w], partner)
-        copy.start()
-        core_copies.append(copy)
+    @pl.when(rank < NB - 1)
+    def _():
+        pl.semaphore_wait(ready, NB - 1 - rank)
+
+    send_roots(False)
 
     strip = pl.ds(pl.multiple_of(k * H, H), H)
     block_copies = {}
@@ -387,6 +384,16 @@
 
     for i in range(NB):
         send_products(1, i, WIDE, WIDE + T)
+
+    for copy in root_copies:
+        copy.wait_recv()
+    loads[4].wait()
+    loads[5].wait()
+    core_copies = []
+    for w, ref in enumerate((lroot, rroot)):
+        copy = remote(ref.at[:, k], ref.at[:, k], core_send.at[w], core_recv.at[w], partner)
+        copy.start()
+        core_copies.append(copy)
 
     for copy in core_copies:
         copy.wait_recv()

time: 44 us -> 44 us (level)
  no operation moved by 1% of the time
where the time goes in v9:
time: 44 us; the launch traced here: 43.9 us
  Pallas kernels  43.2 us (98%)
  between operations  0.67 us (2%)
    pallas_call x1, Pallas kernels, on_device(): pl.pallas_call(kernel, out_shape=(pltpu.VMEM((NB, *products), I16), stat,...  41.7 us
    pallas_call x1, Pallas kernels, on_device(): pl.pallas_call(finish_kernel, out_shape=(stat_out,) * 4 + (jax.ShapeDtype...  1.45 us

profile of v9, /device:TPU:1, one launch (start us, length us, event | category | flops | bytes accessed | tf_op | source)
XLA Modules:
  0.0 43.9 jit_solution(14101437286018911794)
XLA Ops:
  0.6 0.0 copy-start.1
  0.6 0.0 copy-start
  0.7 41.7 %shampoo_step.1 = (s16[8,272,128]{2,1,0:T(8,128)(2,1)S(1)}, f32[8,32,512]{2,1,0:T(8,128)S(1)}, f32[8,32,512]{2,1,0:T(8,128)S(1)}, bf16[512,256]{1,0:T(8,128)(2,1)S(1)}) custom-call(s32[8]{0:T(128)} %home_hbm.1, f32[8,512,256]{2,1,0:T(8,128)} %bitcast.1, bf16[8,32,512]{2,1,0:T(8,128)(2,1)} %lroot_hbm.1, bf16[8,32,512]{2,1,0:T(8,128)(2,1)} %rroot_hbm.1, ...), custom_call_target="tpu_custom_call" | custom-call | flops 2000000000 | bytes 9437184 | tf_op jit(solution)/shard_map/shampoo_step/pallas_call | solution.py:530
  42.4 0.0 copy-done.1
  42.4 0.0 copy-done
  42.4 1.4 %finish_outputs.1 = (f32[8,32,512]{2,1,0:T(8,128)}, f32[8,32,512]{2,1,0:T(8,128)}, f32[8,32,512]{2,1,0:T(8,128)}, f32[8,32,512]{2,1,0:T(8,128)}, bf16[512,256]{1,0:T(8,128)(2,1)}) custom-call(s16[8,272,128]{2,1,0:T(8,128)(2,1)S(1)} %get-tuple-element.9.prod, f32[8,32,512]{2,1,0:T(8,128)S(1)} %copy-done, f32[8,32,512]{2,1,0:T(8,128)S(1)} %copy-done.1, ...), custom_call_target="tpu_custom_call" | custom-call | tf_op jit(solution)/shard_map/finish_outputs/pallas_call | solution.py:548
Async XLA Ops:
  0.6 41.8 %copy-start.1 = (f32[8,32,512]{2,1,0:T(8,128)S(1)}, f32[8,32,512]{2,1,0:T(8,128)}, u32[]{:S(2)}) copy-start(f32[8,32,512]{2,1,0:T(8,128)} %right.1) | copy-start | bytes 1572868
  0.6 41.8 %copy-start = (f32[8,32,512]{2,1,0:T(8,128)S(1)}, f32[8,32,512]{2,1,0:T(8,128)}, u32[]{:S(2)}) copy-start(f32[8,32,512]{2,1,0:T(8,128)} %left.1) | copy-start | bytes 1572868

commit v10 on v9

--- a/solution.py
+++ b/solution.py
@@ -382,8 +382,9 @@
         codes = jnp.concatenate([left_codes[i], code], axis=0)
         prod_out[i, pl.ds(2 * WIDE, T), :] = codes.astype(I32).astype(I16)
 
-    for i in range(NB):
-        send_products(1, i, WIDE, WIDE + T)
+    for i, (a, b) in enumerate(PEERS + [(0, 0)]):
+        if a or not b:
+            send_products(1, i, WIDE, WIDE + T)
 
     for copy in root_copies:
         copy.wait_recv()
@@ -435,6 +436,9 @@
         copy = remote(sums_chip.at[chip_at(a, b)], sums_in.at[i], sum_send.at[i], sum_recv.at[i], along_mp(a, b))
         copy.start()
         sum_copies.append(copy)
+    for i, (a, b) in enumerate(PEERS):
+        if not a:
+            send_products(1, i, WIDE, WIDE + T)
 
     pair_copy.wait_recv()
     total = sums_chip[c]

time: 44 us -> 43.9 us (level)
  no operation moved by 1% of the time
where the time goes in v10:
time: 43.9 us; the launch traced here: 43.8 us
  Pallas kernels  43.1 us (98%)
  between operations  0.67 us (2%)
    pallas_call x1, Pallas kernels, on_device(): pl.pallas_call(kernel, out_shape=(pltpu.VMEM((NB, *products), I16), stat,...  41.7 us
    pallas_call x1, Pallas kernels, on_device(): pl.pallas_call(finish_kernel, out_shape=(stat_out,) * 4 + (jax.ShapeDtype...  1.45 us

profile of v10, /device:TPU:1, one launch (start us, length us, event | category | flops | bytes accessed | tf_op | source)
XLA Modules:
  0.0 43.8 jit_solution(13226427284477010)
XLA Ops:
  0.6 0.0 copy-start.1
  0.6 0.0 copy-start
  0.7 41.7 %shampoo_step.1 = (s16[8,272,128]{2,1,0:T(8,128)(2,1)S(1)}, f32[8,32,512]{2,1,0:T(8,128)S(1)}, f32[8,32,512]{2,1,0:T(8,128)S(1)}, bf16[512,256]{1,0:T(8,128)(2,1)S(1)}) custom-call(s32[8]{0:T(128)} %home_hbm.1, f32[8,512,256]{2,1,0:T(8,128)} %bitcast.1, bf16[8,32,512]{2,1,0:T(8,128)(2,1)} %lroot_hbm.1, bf16[8,32,512]{2,1,0:T(8,128)(2,1)} %rroot_hbm.1, ...), custom_call_target="tpu_custom_call" | custom-call | flops 2000000000 | bytes 9437184 | tf_op jit(solution)/shard_map/shampoo_step/pallas_call | solution.py:534
  42.3 0.0 copy-done.1
  42.3 0.0 copy-done
  42.3 1.4 %finish_outputs.1 = (f32[8,32,512]{2,1,0:T(8,128)}, f32[8,32,512]{2,1,0:T(8,128)}, f32[8,32,512]{2,1,0:T(8,128)}, f32[8,32,512]{2,1,0:T(8,128)}, bf16[512,256]{1,0:T(8,128)(2,1)}) custom-call(s16[8,272,128]{2,1,0:T(8,128)(2,1)S(1)} %get-tuple-element.9.prod, f32[8,32,512]{2,1,0:T(8,128)S(1)} %copy-done, f32[8,32,512]{2,1,0:T(8,128)S(1)} %copy-done.1, ...), custom_call_target="tpu_custom_call" | custom-call | tf_op jit(solution)/shard_map/finish_outputs/pallas_call | solution.py:552
Async XLA Ops:
  0.6 41.7 %copy-start.1 = (f32[8,32,512]{2,1,0:T(8,128)S(1)}, f32[8,32,512]{2,1,0:T(8,128)}, u32[]{:S(2)}) copy-start(f32[8,32,512]{2,1,0:T(8,128)} %right.1) | copy-start | bytes 1572868
  0.6 41.7 %copy-start = (f32[8,32,512]{2,1,0:T(8,128)S(1)}, f32[8,32,512]{2,1,0:T(8,128)}, u32[]{:S(2)}) copy-start(f32[8,32,512]{2,1,0:T(8,128)} %left.1) | copy-start | bytes 1572868

commit v11 on v10

--- a/solution.py
+++ b/solution.py
@@ -132,7 +132,7 @@
     home, part_up, part_down, part_cross, first, second, lroot, rroot,
     ring_out, ring_in, x1_out, x1_in, y2_out, y2_in, x2_out, x2_in,
     work, ghigh, glow, grow_out, grow_in, prod_out, left_codes, pleft, pright,
-    sums_out, sums_other, sums_chip, sums_in, pair_out, pair_in,
+    sums_out, sums_in, pair_out, pair_in,
     load_sem, root_send, root_recv, ring_send, ring_recv, x1_send, x1_recv, s2_send, s2_recv,
     core_send, core_recv, row_send, row_recv, sum_send, sum_recv, store_sem, ready,
 ):
@@ -151,8 +151,8 @@
     def chip_at(a, b):
         return ((xh + a) % 2) * 4 + (z + b) % 4
 
-    def along_mp(a, b):
-        return (d, chip_at(a, b) * 2 + k)
+    def along_mp(a, b, q=0):
+        return (d, chip_at(a, b) * 2 + k + q * (1 - 2 * k))
 
     def remote(src, dst, send, recv, device):
         return pltpu.make_async_remote_copy(
@@ -181,14 +181,16 @@
 
         @pl.when(rank_of(chip_at(a, b)) > rank)
         def _():
-            pl.semaphore_signal(barrier, inc=1, device_id=along_mp(a, b), device_id_type=MESH)
-
-    pl.semaphore_wait(barrier, 5 + rank)
+            for q in range(2):
+                pl.semaphore_signal(barrier, inc=1, device_id=along_mp(a, b, q), device_id_type=MESH)
+
+    pl.semaphore_wait(barrier, 5 + 2 * rank)
     for a, b in PEERS:
 
         @pl.when(rank_of(chip_at(a, b)) < rank)
         def _():
-            pl.semaphore_signal(ready, inc=1, device_id=along_mp(a, b), device_id_type=MESH)
+            for q in range(2):
+                pl.semaphore_signal(ready, inc=1, device_id=along_mp(a, b, q), device_id_type=MESH)
 
     root_copies = []
     for i, (a, b) in enumerate(PEERS):
@@ -289,7 +291,7 @@
 
     @pl.when(rank < NB - 1)
     def _():
-        pl.semaphore_wait(ready, NB - 1 - rank)
+        pl.semaphore_wait(ready, 2 * (NB - 1 - rank))
 
     send_roots(False)
 
@@ -406,12 +408,13 @@
     pright[:, pl.ds(0, H)] = applied
     pair_out[...] = fold(applied * applied)
     n = len(PEERS)
-    pair_copy = remote(pair_out, pair_in, sum_send.at[n], sum_recv.at[n], partner)
+    pair_copy = remote(pair_out, pair_in, sum_send.at[2 * n], sum_recv.at[2 * n], partner)
     pair_copy.start()
 
     loads[6].wait()
     loads[7].wait()
-    for a, b in PEERS + [(0, 0)]:
+    sum_copies = []
+    for i, (a, b) in reversed(list(enumerate(PEERS + [(0, 0)]))):
         slot = chip_at(-a, -b)
         if a or b:
             row_copy(slot, slot).wait_recv()
@@ -425,26 +428,26 @@
             new_second[slot, :, cols] = square
             adam = mean / (jnp.sqrt(square) + ADAM_EPS)
             total = total + fold(adam * adam)
-        sums_out[slot] = total
-
-    chip_copy = remote(sums_out, sums_other, sum_send.at[n + 1], sum_recv.at[n + 1], partner)
-    chip_copy.start()
-    chip_copy.wait_recv()
-    sums_chip[...] = sums_out[...] + sums_other[...]
-    sum_copies = []
-    for i, (a, b) in enumerate(PEERS):
-        copy = remote(sums_chip.at[chip_at(a, b)], sums_in.at[i], sum_send.at[i], sum_recv.at[i], along_mp(a, b))
-        copy.start()
-        sum_copies.append(copy)
+        sums_out[i] = total
+        for q in range(2):
+            if a or b or q:
+                copy = remote(
+                    sums_out.at[i], sums_in.at[2 * i + q], sum_send.at[2 * i + q], sum_recv.at[2 * i + q],
+                    along_mp(-a, -b, q),
+                )
+                copy.start()
+                sum_copies.append(copy)
     for i, (a, b) in enumerate(PEERS):
         if not a:
             send_products(1, i, WIDE, WIDE + T)
 
     pair_copy.wait_recv()
-    total = sums_chip[c]
-    for i, copy in enumerate(sum_copies):
+    for copy in sum_copies:
         copy.wait_recv()
-        total = total + sums_in[i]
+    total = sums_out[n]
+    for i in range(2 * NB):
+        if i != 2 * n:
+            total = total + sums_in[i]
     norms = [jnp.sum(x, axis=(0, 1), keepdims=True) for x in (total, pair_out[...] + pair_in[...])]
     graft = jnp.sqrt(norms[0]) / (jnp.sqrt(norms[1]) + NORM_EPS)
     update[...] = (pright[:, pl.ds(0, H)] * graft).astype(BF16)
@@ -456,7 +459,7 @@
     for copies in (x1_copies, y2_copies, x2_copies, ring, block_copies):
         for copy in copies.values():
             copy.wait_send()
-    for copy in [pair_copy, chip_copy] + root_copies + core_copies + prod_copies + sum_copies:
+    for copy in [pair_copy] + root_copies + core_copies + prod_copies + sum_copies:
         copy.wait_send()
     for store in stores:
         store.wait()
@@ -517,8 +520,8 @@
         pltpu.VMEM((NB, T // 2, LANES), F32),
         pltpu.VMEM((H, B), F32),
         pltpu.VMEM((B, B), F32),
-        *[pltpu.VMEM((NB, 8, LANES), F32)] * 3,
-        pltpu.VMEM((n, 8, LANES), F32),
+        pltpu.VMEM((NB, 8, LANES), F32),
+        pltpu.VMEM((2 * NB, 8, LANES), F32),
         *[pltpu.VMEM((8, LANES), F32)] * 2,
         dma((8,)),
         *[dma((2, n))] * 2,
@@ -527,7 +530,7 @@
         *[dma((5,))] * 2,
         *[dma((8,))] * 2,
         *[dma((3, NB))] * 2,
-        *[dma((n + 2,))] * 2,
+        *[dma((2 * NB,))] * 2,
         dma((2,)),
         pltpu.SemaphoreType.REGULAR,
     ]

time: 43.9 us -> 44.4 us (1.011)
  Pallas kernels: 43.1 us -> 43.6 us
    pallas_call x1, Pallas kernels: 41.7 us -> 42.1 us  [on_device(): pl.pallas_call(kernel, out_shape=(pltpu.VMEM((NB, *products), I16), stat,...]
where the time goes in v11:
time: 44.4 us; the launch traced here: 44.3 us
  Pallas kernels  43.6 us (98%)
  between operations  0.67 us (2%)
    pallas_call x1, Pallas kernels, on_device(): pl.pallas_call(kernel, out_shape=(pltpu.VMEM((NB, *products), I16), stat,...  42.1 us
    pallas_call x1, Pallas kernels, on_device(): pl.pallas_call(finish_kernel, out_shape=(stat_out,) * 4 + (jax.ShapeDtype...  1.45 us

profile of v11, /device:TPU:1, one launch (start us, length us, event | category | flops | bytes accessed | tf_op | source)
XLA Modules:
  0.0 44.3 jit_solution(16961516484801981111)
XLA Ops:
  0.6 0.0 copy-start.1
  0.6 0.0 copy-start
  0.7 42.1 %shampoo_step.1 = (s16[8,272,128]{2,1,0:T(8,128)(2,1)S(1)}, f32[8,32,512]{2,1,0:T(8,128)S(1)}, f32[8,32,512]{2,1,0:T(8,128)S(1)}, bf16[512,256]{1,0:T(8,128)(2,1)S(1)}) custom-call(s32[8]{0:T(128)} %home_hbm.1, f32[8,512,256]{2,1,0:T(8,128)} %bitcast.1, bf16[8,32,512]{2,1,0:T(8,128)(2,1)} %lroot_hbm.1, bf16[8,32,512]{2,1,0:T(8,128)(2,1)} %rroot_hbm.1, ...), custom_call_target="tpu_custom_call" | custom-call | flops 2000000000 | bytes 9437184 | tf_op jit(solution)/shard_map/shampoo_step/pallas_call | solution.py:537
  42.8 0.0 copy-done.1
  42.8 0.0 copy-done
  42.8 1.4 %finish_outputs.1 = (f32[8,32,512]{2,1,0:T(8,128)}, f32[8,32,512]{2,1,0:T(8,128)}, f32[8,32,512]{2,1,0:T(8,128)}, f32[8,32,512]{2,1,0:T(8,128)}, bf16[512,256]{1,0:T(8,128)(2,1)}) custom-call(s16[8,272,128]{2,1,0:T(8,128)(2,1)S(1)} %get-tuple-element.9.prod, f32[8,32,512]{2,1,0:T(8,128)S(1)} %copy-done, f32[8,32,512]{2,1,0:T(8,128)S(1)} %copy-done.1, ...), custom_call_target="tpu_custom_call" | custom-call | tf_op jit(solution)/shard_map/finish_outputs/pallas_call | solution.py:555
Async XLA Ops:
  0.6 42.2 %copy-start.1 = (f32[8,32,512]{2,1,0:T(8,128)S(1)}, f32[8,32,512]{2,1,0:T(8,128)}, u32[]{:S(2)}) copy-start(f32[8,32,512]{2,1,0:T(8,128)} %right.1) | copy-start | bytes 1572868
  0.6 42.2 %copy-start = (f32[8,32,512]{2,1,0:T(8,128)S(1)}, f32[8,32,512]{2,1,0:T(8,128)}, u32[]{:S(2)}) copy-start(f32[8,32,512]{2,1,0:T(8,128)} %left.1) | copy-start | bytes 1572868

commit v12 on v10

--- a/solution.py
+++ b/solution.py
@@ -35,6 +35,7 @@
 TINY = 1e-30
 
 PEERS = [(1, 2), (1, 1), (1, 3), (0, 2), (1, 0), (0, 1), (0, 3)]
+BY_RANK = (0, 4, 1, 5, 2, 6, 3, 7)
 
 
 def code_of(peak):
@@ -266,13 +267,13 @@
                 send_far(w, 1)
     for load in loads[4:]:
         load.start()
-    send_roots(True)
     send_back(1, 0)
     send_back(0, 0)
     send_on(0, 0)
     send_on(1, 0)
     send_back(1, 1)
     send_back(0, 1)
+    send_roots(True)
     send_on(0, 1)
     send_on(1, 1)
     for j in (2, 1, 3):
@@ -409,12 +410,20 @@
     pair_copy = remote(pair_out, pair_in, sum_send.at[n], sum_recv.at[n], partner)
     pair_copy.start()
 
+    for copies in (x1_copies, y2_copies, x2_copies, ring, block_copies):
+        for copy in copies.values():
+            copy.wait_send()
+    for copy in root_copies + core_copies:
+        copy.wait_send()
+
     loads[6].wait()
     loads[7].wait()
-    for a, b in PEERS + [(0, 0)]:
-        slot = chip_at(-a, -b)
-        if a or b:
+    for slot in BY_RANK:
+
+        @pl.when(c != slot)
+        def _():
             row_copy(slot, slot).wait_recv()
+
         total = jnp.zeros((8, LANES), F32)
         scale = scale_of(grow_in[slot, pl.ds(WIDE, T), :])
         for t, grad in enumerate(decode_rows(grow_in.at[slot], 0, scale)):
@@ -453,10 +462,7 @@
         copy.wait_recv()
     for a, b in PEERS:
         row_copy(chip_at(a, b), c).wait_send()
-    for copies in (x1_copies, y2_copies, x2_copies, ring, block_copies):
-        for copy in copies.values():
-            copy.wait_send()
-    for copy in [pair_copy, chip_copy] + root_copies + core_copies + prod_copies + sum_copies:
+    for copy in [pair_copy, chip_copy] + prod_copies + sum_copies:
         copy.wait_send()
     for store in stores:
         store.wait()

time: 43.9 us -> 43.8 us (level)
  no operation moved by 1% of the time
where the time goes in v12:
time: 43.8 us; the launch traced here: 43.7 us
  Pallas kernels  43 us (98%)
  between operations  0.67 us (2%)
    pallas_call x1, Pallas kernels, on_device(): pl.pallas_call(kernel, out_shape=(pltpu.VMEM((NB, *products), I16), stat,...  41.6 us
    pallas_call x1, Pallas kernels, on_device(): pl.pallas_call(finish_kernel, out_shape=(stat_out,) * 4 + (jax.ShapeDtype...  1.45 us

profile of v12, /device:TPU:1, one launch (start us, length us, event | category | flops | bytes accessed | tf_op | source)
XLA Modules:
  0.0 43.7 jit_solution(11747419701454163263)
XLA Ops:
  0.6 0.0 copy-start.1
  0.6 0.0 copy-start
  0.7 41.6 %shampoo_step.1 = (s16[8,272,128]{2,1,0:T(8,128)(2,1)S(1)}, f32[8,32,512]{2,1,0:T(8,128)S(1)}, f32[8,32,512]{2,1,0:T(8,128)S(1)}, bf16[512,256]{1,0:T(8,128)(2,1)S(1)}) custom-call(s32[8]{0:T(128)} %home_hbm.1, f32[8,512,256]{2,1,0:T(8,128)} %bitcast.1, bf16[8,32,512]{2,1,0:T(8,128)(2,1)} %lroot_hbm.1, bf16[8,32,512]{2,1,0:T(8,128)(2,1)} %rroot_hbm.1, ...), custom_call_target="tpu_custom_call" | custom-call | flops 2000000000 | bytes 9437184 | tf_op jit(solution)/shard_map/shampoo_step/pallas_call | solution.py:540
  42.2 0.0 copy-done.1
  42.2 0.0 copy-done
  42.3 1.4 %finish_outputs.1 = (f32[8,32,512]{2,1,0:T(8,128)}, f32[8,32,512]{2,1,0:T(8,128)}, f32[8,32,512]{2,1,0:T(8,128)}, f32[8,32,512]{2,1,0:T(8,128)}, bf16[512,256]{1,0:T(8,128)(2,1)}) custom-call(s16[8,272,128]{2,1,0:T(8,128)(2,1)S(1)} %get-tuple-element.9.prod, f32[8,32,512]{2,1,0:T(8,128)S(1)} %copy-done, f32[8,32,512]{2,1,0:T(8,128)S(1)} %copy-done.1, ...), custom_call_target="tpu_custom_call" | custom-call | tf_op jit(solution)/shard_map/finish_outputs/pallas_call | solution.py:558
Async XLA Ops:
  0.6 41.6 %copy-start.1 = (f32[8,32,512]{2,1,0:T(8,128)S(1)}, f32[8,32,512]{2,1,0:T(8,128)}, u32[]{:S(2)}) copy-start(f32[8,32,512]{2,1,0:T(8,128)} %right.1) | copy-start | bytes 1572868
  0.6 41.6 %copy-start = (f32[8,32,512]{2,1,0:T(8,128)S(1)}, f32[8,32,512]{2,1,0:T(8,128)}, u32[]{:S(2)}) copy-start(f32[8,32,512]{2,1,0:T(8,128)} %left.1) | copy-start | bytes 1572868
